TPU v7x, 256 devices: a whole 4x4x8 slice. The times are simulated.
256 devices in a mesh: blk: 16 (over y_hi, z), frames: 16 (over x, y_lo, core).
Axes of the slice: x: 4, y: 4 (y_hi: 2, y_lo: 2; y = y_hi * 2 + y_lo), z: 8, core: 2. Of those that a mesh axis runs over, the one named last changes fastest.
Arguments:
- coarse_query: bfloat16 [512, 16, 256], P('blk'), may hold values from -125 to 125
- coarse_feat: bfloat16 [64, 8160, 256], P('frames', 'blk'), may hold values from -61 to 61
- fine_query: bfloat16 [512, 128], P(('blk', 'frames')), may hold values from -175 to 175
- fine_tiles: bfloat16 [64, 1024, 64, 128], P('frames', 'blk'), may hold values from -61 to 61
- track_pos: int32 [2, 64, 512], P(None, None, ('blk', 'frames')), may hold values from 0 to 959, as said below
- tile_list: int32 [64, 16, 16, 8], P('frames', 'blk'), may hold values from 0 to 63, as said below
- tile_valid: int32 [64, 16, 16, 8], P('frames', 'blk'), may hold values from 0 to 1, as said below
Outputs:
- coarse_pos: float32 [2, 64, 512], P(None, 'frames', 'blk')
- fine_offset: float32 [2, 64, 512], P(None, None, ('blk', 'frames'))
Inputs may be any that keep to these rules, and one draw needn't show every extreme that they name: `tile_list`: in each list the valid slots come first and name distinct tiles of the group's window; padded slots hold 63; in every frame and group some owner's list is full. `tile_valid`: each list has at least 4 valid slots. `track_pos`: rows lie below 544 and columns below 960.
All inputs are finite; a program needn't handle non-finite values.
Results may differ from a plain program's by a relative error of at most 0.0003.
Values may be sent and summed in bfloat16 or wider, within the bound.
A program may use at most 192 MiB of HBM per device.

v0:
```python
import math

import jax
import jax.numpy as jnp
from jax import lax
from jax.sharding import PartitionSpec as P

GH = 68
GW = 120
TILE = 8


spread_cells = 32.0


def refine_frame(descriptors, tile_block, tile_ids, tile_live, track_row, track_col, base_cell):
    slot_count, cell_count, channels = tile_block.shape
    flat_tiles = tile_block.reshape(slot_count * cell_count, channels)
    scores = jnp.einsum(
        "nc,kc->nk", descriptors, flat_tiles, preferred_element_type=jnp.float32
    ) * (1.0 / math.sqrt(channels))
    global_cell = base_cell + tile_ids
    inner_cell = jnp.arange(cell_count, dtype=jnp.int32)
    cell_row = (global_cell // GW * TILE)[:, None] + (inner_cell // TILE)[None, :]
    cell_col = (global_cell % GW * TILE)[:, None] + (inner_cell % TILE)[None, :]
    cell_row = cell_row.reshape(-1).astype(jnp.float32)
    cell_col = cell_col.reshape(-1).astype(jnp.float32)
    distance = (cell_row[None, :] - track_row[:, None]) ** 2 + (
        cell_col[None, :] - track_col[:, None]
    ) ** 2
    scores = scores - distance * (0.5 / (spread_cells * spread_cells))
    live_cells = jnp.broadcast_to(tile_live[:, None] > 0, (slot_count, cell_count)).reshape(-1)
    scores = jnp.where(live_cells[None, :], scores, -1e30)
    highest = jnp.max(scores, axis=1, keepdims=True)
    weights = jnp.exp(scores - highest)
    totals = jnp.sum(weights, axis=1)
    mean_row = jnp.sum(weights * cell_row[None, :], axis=1) / totals
    mean_col = jnp.sum(weights * cell_col[None, :], axis=1) / totals
    return ((mean_row - track_row) / spread_cells, (mean_col - track_col) / spread_cells)


def coarse_finish(row_mean, col_mean):
    row_heads = jnp.mean(row_mean, axis=2)
    col_heads = jnp.mean(col_mean, axis=2)
    return jnp.stack(
        [(row_heads - (GH - 1) / 2.0) / (GH / 4.0), (col_heads - (GW - 1) / 2.0) / (GW / 4.0)]
    )


def body(coarse_query, coarse_feat, fine_query, fine_tiles, track_pos, tile_list, tile_valid):
    track_group, heads, channels = coarse_query.shape
    frames_here, region, _ = coarse_feat.shape
    scale = 1.0 / math.sqrt(channels)
    group_start = lax.axis_index("blk") * region
    query_rows = coarse_query.reshape(track_group * heads, channels)
    row_count = query_rows.shape[0]
    zeros_state = jnp.zeros((frames_here, row_count), jnp.float32)
    shard_piece = lax.all_gather(coarse_feat, "blk", axis=1, tiled=True)
    first_pos = jnp.int32(0)
    maxima = jnp.full((frames_here, row_count), -jnp.inf, jnp.float32)
    totals = zeros_state
    row_sums = zeros_state
    col_sums = zeros_state
    length = shard_piece.shape[1]
    for offset in range(0, length, 512):
        feat_block = shard_piece[:, offset : offset + 512]
        scores = (
            jnp.einsum("rc,fpc->frp", query_rows, feat_block, preferred_element_type=jnp.float32)
            * scale
        )
        positions = first_pos + offset + jnp.arange(feat_block.shape[1], dtype=jnp.int32)
        pos_row = (positions // GW).astype(jnp.float32)
        pos_col = (positions % GW).astype(jnp.float32)
        new_max = jnp.maximum(maxima, jnp.max(scores, axis=2))
        retain = jnp.exp(maxima - new_max)
        weights = jnp.exp(scores - new_max[:, :, None])
        totals = totals * retain + jnp.sum(weights, axis=2)
        row_sums = row_sums * retain + jnp.sum(weights * pos_row[None, None, :], axis=2)
        col_sums = col_sums * retain + jnp.sum(weights * pos_col[None, None, :], axis=2)
        maxima = new_max
    final_state = (maxima, totals, row_sums, col_sums)
    row_mean = (final_state[2] / final_state[1]).reshape(frames_here, track_group, heads)
    col_mean = (final_state[3] / final_state[1]).reshape(frames_here, track_group, heads)
    coarse_pos = coarse_finish(row_mean, col_mean)
    list_ids = jnp.transpose(tile_list[:, 0], (1, 0, 2))
    list_live = jnp.transpose(tile_valid[:, 0], (1, 0, 2))
    picked = fine_tiles[jnp.arange(frames_here, dtype=jnp.int32)[None, :, None], list_ids]
    per_frame = jax.vmap(refine_frame, in_axes=(None, 0, 0, 0, 0, 0, None))
    got_tiles, got_ids, got_live = (
        lax.all_to_all(picked, "frames", split_axis=0, concat_axis=0, tiled=True),
        lax.all_to_all(list_ids, "frames", split_axis=0, concat_axis=0, tiled=True),
        lax.all_to_all(list_live, "frames", split_axis=0, concat_axis=0, tiled=True),
    )
    window = got_tiles.shape[0] * got_tiles.shape[1]
    got_tiles = got_tiles.reshape((window,) + got_tiles.shape[2:])
    got_ids = got_ids.reshape(window, -1)
    got_live = got_live.reshape(window, -1)
    places = track_pos.astype(jnp.float32)
    rows_out, cols_out = per_frame(
        fine_query, got_tiles, got_ids, got_live, places[0], places[1], group_start
    )
    fine_offset = jnp.stack([rows_out, cols_out])
    return (coarse_pos, fine_offset)


def solution(mesh):
    return jax.shard_map(
        body,
        mesh=mesh,
        in_specs=(
            P("blk", None, None),
            P("frames", "blk", None),
            P(("blk", "frames"), None),
            P("frames", "blk", None, None),
            P(None, None, ("blk", "frames")),
            P("frames", "blk", None, None),
            P("frames", "blk", None, None),
        ),
        out_specs=(P(None, "frames", "blk"), P(None, None, ("blk", "frames"))),
        check_vma=False,
    )
```

profile of v0, /device:TPU:1, one launch (start us, length us, event | category | flops | bytes accessed | tf_op | source)
XLA Modules:
  0.0 419.7 jit_solution(9521634388056625112)
XLA Ops:
  9.3 6.8 %all-to-all-start.2 = ((s32[16,4,8]{2,1,0:T(4,128)}), s32[16,4,8]{2,1,0:T(4,128)S(1)}, u32[]{:S(2)}, u32[]{:S(2)}) async-start(s32[16,4,8]{2,1,0:T(4,128)} %bitcast.25), calls=%async_computation.2 | async-start | bytes 65536 | tf_op jit(solution)/shard_map/all_to_all | solution.py:91
  17.5 4.4 %all-to-all-done.2 = s32[16,4,8]{2,1,0:T(4,128)S(1)} async-done(((s32[16,4,8]{2,1,0:T(4,128)}), s32[16,4,8]{2,1,0:T(4,128)S(1)}, u32[]{:S(2)}, u32[]{:S(2)}) %all-to-all-start.2) | async-done | bytes 2080 | tf_op jit(solution)/shard_map/all_to_all | solution.py:91
  22.0 3.7 all-to-all-start
  26.5 10.3 %gather_fusion = bf16[512,64,128]{2,1,0:T(8,128)(2,1)} fusion(bf16[4,64,64,128]{3,2,1,0:T(8,128)(2,1)} %param.10, s32[512]{0:T(512)S(1)} %reshape.890), kind=kCustom, calls=%fused_computation | custom fusion | bytes 16781312 | tf_op jit(solution)/shard_map/gather | solution.py:87
  36.8 5.9 %all-to-all-start.1 = ((bf16[16,4,8,64,128]{4,3,2,1,0:T(8,128)(2,1)}), bf16[16,4,8,64,128]{4,3,2,1,0:T(8,128)(2,1)}, u32[]{:S(2)}, u32[]{:S(2)}) async-start(bf16[16,4,8,64,128]{4,3,2,1,0:T(8,128)(2,1)} %bitcast.260), calls=%async_computation.1 | async-start | bytes 16777216 | tf_op jit(solution)/shard_map/all_to_all | solution.py:90
  44.4 129.9 %all-to-all-done.1 = bf16[16,4,8,64,128]{4,3,2,1,0:T(8,128)(2,1)} async-done(((bf16[16,4,8,64,128]{4,3,2,1,0:T(8,128)(2,1)}), bf16[16,4,8,64,128]{4,3,2,1,0:T(8,128)(2,1)}, u32[]{:S(2)}, u32[]{:S(2)}) %all-to-all-start.1) | async-done | bytes 8388640 | tf_op jit(solution)/shard_map/all_to_all | solution.py:90
  174.3 5.8 %multiply_reduce_fusion.33 = (f32[64,2]{1,0:T(8,128)S(1)}, f32[64,2]{1,0:T(8,128)S(1)}, f32[64,2]{1,0:T(8,128)S(1)}) fusion(f32[64,512]{1,0:T(8,128)S(1)} %get-tuple-element.151, f32[64,512]{1,0:T(8,128)S(1)} %get-tuple-element.150, bf16[64,512,128]{2,1,0:T(8,128)(2,1)} %bitcast.29, pred[64,512]{1,0:T(8,128)(4,1)S(1)} %broadcast_in_dim.23, ...), kind=kOutput, calls=%fused_computation.137 | convolution fusion | flops 17760512 | bytes 8686592 | tf_op jit(solution)/shard_map/vmap()/sub | solution.py:35
  180.9 113.8 %all-gather.2.cloned.1.call-done = bf16[4,8160,256]{2,0,1:T(4,128)(2,1)} async-done(((bf16[4,510,256]{2,0,1:T(4,128)(2,1)}), bf16[4,8160,256]{2,0,1:T(4,128)(2,1)}) %all-gather.2.cloned.1.call-update) | async-done | bytes 16711696 | tf_op jit(solution)/shard_map/all_gather | solution.py:58
  298.8 10.1 %fusion.197 = (bf16[4,512,256]{2,0,1:T(4,128)(2,1)S(1)}, bf16[4,512,256]{2,0,1:T(4,128)(2,1)S(1)}, bf16[4,512,256]{2,0,1:T(4,128)(2,1)S(1)}, bf16[4,512,256]{2,0...) fusion(bf16[4,8160,256]{2,0,1:T(4,128)(2,1)} %all-gather.2.clon, ...), kind=kLoop, calls=%fused_computation.377 | loop fusion | bytes 31457280 | tf_op jit(solution)/shard_map/slice | solution.py:66
  308.9 2.7 bitcast_reduce_fusion
  311.6 2.7 bitcast_reduce_fusion.1
  314.4 2.7 bitcast_reduce_fusion.2
  317.1 2.7 bitcast_reduce_fusion.3
  319.7 2.7 bitcast_reduce_fusion.4
  322.5 2.7 bitcast_reduce_fusion.5
  325.2 2.7 bitcast_reduce_fusion.6
  327.9 2.8 bitcast_reduce_fusion.7
  330.7 2.7 bitcast_reduce_fusion.8
  336.1 2.7 bitcast_reduce_fusion.10
  338.7 2.8 bitcast_reduce_fusion.11
  341.5 2.7 bitcast_reduce_fusion.12
  344.2 2.7 bitcast_reduce_fusion.14
  346.9 2.7 bitcast_reduce_fusion.13
  351.1 3.9 multiply_reduce_fusion.31
  355.1 6.8 %multiply_reduce_fusion.15 = (f32[4,512]{1,0:T(4,128)S(1)}, f32[4,512]{1,0:T(4,128)S(1)}, f32[4,512]{1,0:T(4,128)S(1)}, f32[4,512]{1,0:T(4,128)S(1)}, f32[4,512]{1,0:T(4,128)S(1)}, /*index=5*/f32[4,512]{1,0:T(4,128)S(1)}) fusion(f32[4,512,512]{2,1,0:T(8,128)} %get-tuple-element.96, f32[512]{0:T(512)S(1)} %fusion.108, f32[4,512]{1,0:T(4,128)S(1)} %get-tuple-element.54, ...), kind=kLoop, calls=%fused_computation.62 | loop fusion | flops 14667776 | bytes 8462336 | tf_op jit(solution)/shard_map/reduce_sum | solution.py:78
  362.0 6.8 %multiply_reduce_fusion.17 = (f32[4,512]{1,0:T(4,128)S(1)}, f32[4,512]{1,0:T(4,128)S(1)}, f32[4,512]{1,0:T(4,128)S(1)}, f32[4,512]{1,0:T(4,128)S(1)}, f32[4,512]{1,0:T(4,128)S(1)}, /*index=5*/f32[4,512]{1,0:T(4,128)S(1)}) fusion(f32[4,512,512]{2,1,0:T(8,128)} %get-tuple-element.100, f32[512]{0:T(512)S(1)} %fusion.116, f32[4,512]{1,0:T(4,128)S(1)} %get-tuple-element.56, ...), kind=kLoop, calls=%fused_computation.64 | loop fusion | flops 14667776 | bytes 8462336 | tf_op jit(solution)/shard_map/reduce_sum | solution.py:78
  369.0 6.8 %multiply_reduce_fusion.19 = (f32[4,512]{1,0:T(4,128)S(1)}, f32[4,512]{1,0:T(4,128)S(1)}, f32[4,512]{1,0:T(4,128)S(1)}, f32[4,512]{1,0:T(4,128)S(1)}, f32[4,512]{1,0:T(4,128)S(1)}, /*index=5*/f32[4,512]{1,0:T(4,128)S(1)}) fusion(f32[4,512,512]{2,1,0:T(8,128)} %get-tuple-element.104, f32[512]{0:T(512)S(1)} %fusion.124, f32[4,512]{1,0:T(4,128)S(1)} %get-tuple-element.58, ...), kind=kLoop, calls=%fused_computation.66 | loop fusion | flops 14667776 | bytes 8462336 | tf_op jit(solution)/shard_map/reduce_sum | solution.py:78
  376.0 6.8 %multiply_reduce_fusion.21 = (f32[4,512]{1,0:T(4,128)S(1)}, f32[4,512]{1,0:T(4,128)S(1)}, f32[4,512]{1,0:T(4,128)S(1)}, f32[4,512]{1,0:T(4,128)S(1)}, f32[4,512]{1,0:T(4,128)S(1)}, /*index=5*/f32[4,512]{1,0:T(4,128)S(1)}) fusion(f32[4,512,512]{2,1,0:T(8,128)} %get-tuple-element.108, f32[512]{0:T(512)S(1)} %fusion.132, f32[4,512]{1,0:T(4,128)S(1)} %get-tuple-element.60, ...), kind=kLoop, calls=%fused_computation.68 | loop fusion | flops 14667776 | bytes 8462336 | tf_op jit(solution)/shard_map/reduce_sum | solution.py:78
  382.9 7.0 %multiply_reduce_fusion.23 = (f32[4,512]{1,0:T(4,128)S(1)}, f32[4,512]{1,0:T(4,128)S(1)}, f32[4,512]{1,0:T(4,128)S(1)}, f32[4,512]{1,0:T(4,128)S(1)}, f32[4,512]{1,0:T(4,128)S(1)}, /*index=5*/f32[4,512]{1,0:T(4,128)S(1)}) fusion(f32[4,512,512]{2,1,0:T(8,128)} %get-tuple-element.112, f32[512]{0:T(512)S(1)} %fusion.140, f32[4,512]{1,0:T(4,128)S(1)} %get-tuple-element.62, ...), kind=kLoop, calls=%fused_computation.70 | loop fusion | flops 14667776 | bytes 8462336 | tf_op jit(solution)/shard_map/reduce_sum | solution.py:78
  390.1 6.8 %multiply_reduce_fusion.25 = (f32[4,512]{1,0:T(4,128)S(1)}, f32[4,512]{1,0:T(4,128)S(1)}, f32[4,512]{1,0:T(4,128)S(1)}, f32[4,512]{1,0:T(4,128)S(1)}, f32[4,512]{1,0:T(4,128)S(1)}, /*index=5*/f32[4,512]{1,0:T(4,128)S(1)}) fusion(f32[4,512,512]{2,1,0:T(8,128)} %get-tuple-element.116, f32[512]{0:T(512)S(1)} %fusion.148, f32[4,512]{1,0:T(4,128)S(1)} %get-tuple-element.64, ...), kind=kLoop, calls=%fused_computation.72 | loop fusion | flops 14667776 | bytes 8462336 | tf_op jit(solution)/shard_map/reduce_sum | solution.py:78
  397.1 6.8 %multiply_reduce_fusion.27 = (f32[4,512]{1,0:T(4,128)S(1)}, f32[4,512]{1,0:T(4,128)S(1)}, f32[4,512]{1,0:T(4,128)S(1)}, f32[4,512]{1,0:T(4,128)S(1)}, f32[4,512]{1,0:T(4,128)S(1)}, /*index=5*/f32[4,512]{1,0:T(4,128)S(1)}) fusion(f32[4,512,512]{2,1,0:T(8,128)} %get-tuple-element.120, f32[512]{0:T(512)S(1)} %fusion.156, f32[4,512]{1,0:T(4,128)S(1)} %get-tuple-element.66, ...), kind=kLoop, calls=%fused_computation.74 | loop fusion | flops 14667776 | bytes 8462336 | tf_op jit(solution)/shard_map/reduce_sum | solution.py:78
  404.0 3.8 multiply_reduce_fusion.29
  (142 shorter events, 20.4 us)
Async XLA Ops:
  7.2 289.1 %copy-start = (bf16[32,16,256]{2,1,0:T(8,128)(2,1)S(1)}, bf16[32,16,256]{2,1,0:T(8,128)(2,1)}, u32[]{:S(2)}) copy-start(bf16[32,16,256]{2,1,0:T(8,128)(2,1)} %param.7) | copy-start | bytes 786436
  7.2 287.5 %all-gather.2.cloned.1.call-start = ((), (), s32[]{:S(2)}) async-start(), calls=%async_computation.3 | async-start | bytes 17756160 | tf_op jit(solution)/shard_map/all_gather | solution.py:58
  9.3 12.7 %all-to-all-start.2 = ((s32[16,4,8]{2,1,0:T(4,128)}), s32[16,4,8]{2,1,0:T(4,128)S(1)}, u32[]{:S(2)}, u32[]{:S(2)}) async-start(s32[16,4,8]{2,1,0:T(4,128)} %bitcast.25), calls=%async_computation.2 | async-start | bytes 65536 | tf_op jit(solution)/shard_map/all_to_all | solution.py:91
  22.0 14.8 %all-to-all-start = ((s32[16,4,8]{2,1,0:T(4,128)}), s32[16,4,8]{2,1,0:T(4,128)S(1)}, u32[]{:S(2)}, u32[]{:S(2)}) async-start(s32[16,4,8]{2,1,0:T(4,128)} %bitcast.22), calls=%async_computation | async-start | bytes 65536 | tf_op jit(solution)/shard_map/all_to_all | solution.py:92
  36.8 6.1 %copy-start.1 = (s32[2,64,2]{1,2,0:T(2,128)S(1)}, s32[2,64,2]{1,2,0:T(2,128)}, u32[]{:S(2)}) copy-start(s32[2,64,2]{1,2,0:T(2,128)} %param.11) | copy-start | bytes 3076
  36.8 137.5 %copy-start.2 = (bf16[2,128]{1,0:T(2,128)(2,1)S(1)}, bf16[2,128]{1,0:T(2,128)(2,1)}, u32[]{:S(2)}) copy-start(bf16[2,128]{1,0:T(2,128)(2,1)} %param.9) | copy-start | bytes 1540
  36.8 137.5 %all-to-all-start.1 = ((bf16[16,4,8,64,128]{4,3,2,1,0:T(8,128)(2,1)}), bf16[16,4,8,64,128]{4,3,2,1,0:T(8,128)(2,1)}, u32[]{:S(2)}, u32[]{:S(2)}) async-start(bf16[16,4,8,64,128]{4,3,2,1,0:T(8,128)(2,1)} %bitcast.260), calls=%async_computation.1 | async-start | bytes 16777216 | tf_op jit(solution)/shard_map/all_to_all | solution.py:90
Sparse Core Ops, SparseCore 0:
  10.7 283.9 all-gather.1
where the time goes:
time: 426 us; the launch traced here: 420 us
  waiting for transfers between devices  249 us (58%)
  other arithmetic  58.7 us (14%)
  matrix products  49.1 us (12%)
  local copies, waits for them, and re-layouts  31.4 us (7%)
  starting transfers between devices  16.4 us (4%)
  between operations  15.2 us (4%)
    all_to_all x1, waiting for transfers between devices, body(): lax.all_to_all(picked, 'frames', split_axis=0, concat_axis=0, tiled=True)  130 us
    all_gather x1, waiting for transfers between devices, body(): shard_piece = lax.all_gather(coarse_feat, 'blk', axis=1, tiled=True)  114 us
    reduce_sum x9, other arithmetic, body(): jnp.sum(weights * pos_row[None, None, :], axis=2)  55.3 us
    dot_general x16, matrix products, body(): jnp.einsum('rc,fpc->frp', query_rows, feat_block, preferred_element_type=...  43.3 us
    slice x2, local copies, waits for them, and re-layouts, body(): feat_block = shard_piece[:, offset:offset + 512]  11.6 us
    gather x1, local copies, waits for them, and re-layouts, body(): fine_tiles[jnp.arange(frames_here, dtype=jnp.int32)[None, :, None], list_...  10.3 us
  transfers between devices with their start and end apart: 4, of which 3 were waited for; matrix products, arithmetic and copies ran while one was open for 5% of the time, Pallas kernels for 0%

commit v1 on v0

v1 whole, which is shorter than its diff:
```python
import math

import jax
import jax.numpy as jnp
from jax import lax
from jax.sharding import PartitionSpec as P

GH = 68
GW = 120
TILE = 8
SPREAD = 32.0


def coarse(coarse_query, coarse_feat):
    track_group, heads, channels = coarse_query.shape
    frames_here, region, _ = coarse_feat.shape
    blocks = lax.axis_size("blk")
    scale = 1.0 / math.sqrt(channels)
    start = lax.axis_index("blk") * region
    queries = lax.all_gather(
        coarse_query.reshape(track_group * heads, channels), "blk", axis=0
    )
    positions = start + jnp.arange(region, dtype=jnp.int32)
    pos_row = (positions // GW).astype(jnp.float32)
    pos_col = (positions % GW).astype(jnp.float32)
    scores = (
        jnp.einsum("brc,fpc->bfpr", queries, coarse_feat, preferred_element_type=jnp.float32)
        * scale
    )
    top = jnp.max(scores, axis=2)
    weights = jnp.exp(scores - top[:, :, None])
    stats = jnp.stack(
        [
            top,
            jnp.sum(weights, axis=2),
            jnp.sum(weights * pos_row[None, None, :, None], axis=2),
            jnp.sum(weights * pos_col[None, None, :, None], axis=2),
        ],
        axis=1,
    )
    stats = lax.all_to_all(stats, "blk", split_axis=0, concat_axis=0, tiled=True)
    top = jnp.max(stats[:, 0], axis=0, keepdims=True)
    factor = jnp.exp(stats[:, 0] - top)
    total = jnp.sum(stats[:, 1] * factor, axis=0)
    rows = jnp.sum(stats[:, 2] * factor, axis=0) / total
    cols = jnp.sum(stats[:, 3] * factor, axis=0) / total
    rows = jnp.mean(rows.reshape(frames_here, track_group, heads), axis=2)
    cols = jnp.mean(cols.reshape(frames_here, track_group, heads), axis=2)
    return jnp.stack(
        [(rows - (GH - 1) / 2.0) / (GH / 4.0), (cols - (GW - 1) / 2.0) / (GW / 4.0)]
    )


def fine(fine_query, fine_tiles, track_pos, tile_list, tile_valid, region):
    frames_here, tiles, cells, channels = fine_tiles.shape
    owners = tile_list.shape[2]
    owned = fine_query.shape[0]
    start = lax.axis_index("blk") * region
    descs = lax.all_gather(fine_query, "frames", axis=0, tiled=True)
    places = lax.all_to_all(
        track_pos, "frames", split_axis=1, concat_axis=2, tiled=True
    ).astype(jnp.float32)
    scores = jnp.einsum(
        "nc,fkc->fnk",
        descs,
        fine_tiles.reshape(frames_here, tiles * cells, channels),
        preferred_element_type=jnp.float32,
    ) * (1.0 / math.sqrt(channels))
    ids = tile_list[:, 0]
    live = tile_valid[:, 0]
    listed = jnp.any(
        (ids[:, :, :, None] == jnp.arange(tiles)) & (live[:, :, :, None] > 0), axis=2
    )
    listed = jnp.repeat(jnp.repeat(listed, owned, axis=1), cells, axis=2)
    index = jnp.arange(tiles * cells, dtype=jnp.int32)
    cell = start + index // cells
    inner = index % cells
    row = (cell // GW * TILE + inner // TILE).astype(jnp.float32)
    col = (cell % GW * TILE + inner % TILE).astype(jnp.float32)
    away_row = row - places[0][:, :, None]
    away_col = col - places[1][:, :, None]
    scores = scores - (away_row**2 + away_col**2) * (0.5 / (SPREAD * SPREAD))
    scores = jnp.where(listed, scores, -1e30)
    weights = jnp.exp(scores - jnp.max(scores, axis=2, keepdims=True))
    total = jnp.sum(weights, axis=2)
    out = jnp.stack(
        [
            jnp.sum(weights * away_row, axis=2) / total / SPREAD,
            jnp.sum(weights * away_col, axis=2) / total / SPREAD,
        ]
    )
    return lax.all_to_all(out, "frames", split_axis=2, concat_axis=1, tiled=True)


def body(coarse_query, coarse_feat, fine_query, fine_tiles, track_pos, tile_list, tile_valid):
    offset = fine(
        fine_query, fine_tiles, track_pos, tile_list, tile_valid, coarse_feat.shape[1]
    )
    return (coarse(coarse_query, coarse_feat), offset)


def solution(mesh):
    return jax.shard_map(
        body,
        mesh=mesh,
        in_specs=(
            P("blk", None, None),
            P("frames", "blk", None),
            P(("blk", "frames"), None),
            P("frames", "blk", None, None),
            P(None, None, ("blk", "frames")),
            P("frames", "blk", None, None),
            P("frames", "blk", None, None),
        ),
        out_specs=(P(None, "frames", "blk"), P(None, None, ("blk", "frames"))),
        check_vma=False,
    )
```

time: 426 us -> 203 us (0.48)
  the two profiles are of different devices: /device:TPU:1 before, /device:TPU:14 now
where the time goes in v1:
time: 203 us
  waiting for transfers between devices  76.4 us (38%)
  other arithmetic  38.6 us (19%)
  matrix products  30 us (15%)
  starting transfers between devices  18.9 us (9%)
  blocking collectives  15.4 us (8%)
  between operations  14.2 us (7%)
  local copies, waits for them, and re-layouts  9.39 us (5%)
    all_gather x1, waiting for transfers between devices, coarse(): lax.all_gather(coarse_query.reshape(track_group * heads, channels), 'blk'...  62.3 us
    reduce_sum x1, other arithmetic, coarse(): jnp.sum(weights, axis=2)  36.5 us
    dot_general x1, matrix products, coarse(): jnp.einsum('brc,fpc->bfpr', queries, coarse_feat, preferred_element_type=...  25.3 us
    all_gather x1, blocking collectives, fine(): descs = lax.all_gather(fine_query, 'frames', axis=0, tiled=True)  15.4 us
    all_to_all x1, waiting for transfers between devices, coarse(): lax.all_to_all(stats, 'blk', split_axis=0, concat_axis=0, tiled=True)  13.4 us
    all_to_all x1, starting transfers between devices, fine(): lax.all_to_all(out, 'frames', split_axis=2, concat_axis=1, tiled=True)  8.1 us
    all_to_all x1, starting transfers between devices, fine(): lax.all_to_all(track_pos, 'frames', split_axis=1, concat_axis=2, tiled=True)  5.7 us
    all_to_all x1, starting transfers between devices, coarse(): lax.all_to_all(stats, 'blk', split_axis=0, concat_axis=0, tiled=True)  5.03 us
  transfers between devices with their start and end apart: 4, of which 2 were waited for; matrix products, arithmetic and copies ran while one was open for 38% of the time, Pallas kernels for 0%

profile of v1, /device:TPU:14, one launch (start us, length us, event | category | flops | bytes accessed | tf_op | source)
XLA Modules:
  0.0 202.8 jit_solution(1856049340781756826)
XLA Ops:
  7.2 0.0 all-gather.3.cloned.1.call-start
  7.2 0.7 all-gather.3.cloned.1.call-update
  7.9 1.4 copy.87
  9.3 5.7 %all-to-all-start.1 = ((s32[2,64,2]{2,0,1:T(2,128)}), s32[2,64,2]{2,0,1:T(2,128)S(1)}, u32[]{:S(2)}, u32[]{:S(2)}) async-start(s32[2,64,2]{2,0,1:T(2,128)} %copy.87), calls=%async_computation.1 | async-start | bytes 131072 | tf_op jit(solution)/shard_map/all_to_all | solution.py:60
  15.0 0.8 copy.83
  15.8 0.7 compare_bitcast_fusion
  16.5 0.1 copy.84
  16.7 0.2 fusion.16
  16.9 15.4 %all-gather = bf16[16,2,128]{2,1,0:T(2,128)(2,1)S(1)} all-gather(bf16[1,2,128]{2,1,0:T(2,128)(2,1)} %bitcast.111), channel_id=1, replica_groups=mesh['blk'=16,'frames'=16] {'frames'}, dimensions={0}, use_global_device_ids=true | all-gather | bytes 8704 | tf_op jit(solution)/shard_map/all_gather | solution.py:59
  32.3 1.4 broadcast_in_dim.9
  33.7 2.6 %reshape.202 = pred[4,32,4096]{2,1,0:T(32,128)(4,1)S(1)} reshape(pred[4,32,64,64]{3,2,1,0:T(32,128)(4,1)S(1)} %broadcast_in_dim.9) | data formatting | bytes 1048576 | tf_op jit(solution)/shard_map/reshape | solution.py:74
  36.4 0.0 all-to-all-done.1
  36.4 0.1 copy.88
  36.5 0.1 convert_element_type.42
  36.6 0.1 copy.90
  36.7 0.1 copy.92
  36.8 4.6 %fusion.12 = (f32[4,32]{1,0:T(4,128)S(1)}, f32[4,32]{1,0:T(4,128)S(1)}, f32[4,32]{1,0:T(4,128)S(1)}) fusion(f32[4,32]{1,0:T(4,128)S(1)} %copy.90, f32[4096]{0:T(1024)S(1)} %get-tuple-element.19, f32[4,32]{1,0:T(4,128)S(1)} %copy.92, f32[4096]{0:T(1024)S(1)} %get-tuple-element.20, pred[4,32,4096]{2,1,0:T(32,128)(4,1)S(1)} %reshape.202, ...), kind=kOutput, calls=%fused_computation.21 | convolution fusion | flops 143134464 | bytes 4762112 | tf_op jit(solution)/shard_map/sub | solution.py:84
  41.4 0.7 copy.93
  42.1 8.1 %all-to-all-start.2 = ((f32[2,4,32]{1,0,2:T(2,128)}), f32[2,4,32]{1,0,2:T(2,128)S(1)}, u32[]{:S(2)}, u32[]{:S(2)}) async-start(f32[2,4,32]{1,0,2:T(2,128)} %copy.93), calls=%async_computation.2 | async-start | bytes 65536 | tf_op jit(solution)/shard_map/all_to_all | solution.py:92
  50.2 62.3 %all-gather.3.cloned.1.call-done = bf16[16,512,256]{2,1,0:T(8,128)(2,1)} async-done(((bf16[1,512,256]{2,1,0:T(8,128)(2,1)}), bf16[16,512,256]{2,1,0:T(8,128)(2,1)}) %all-gather.3.cloned.1.call-update) | async-done | bytes 4194320 | tf_op jit(solution)/shard_map/all_gather | solution.py:20
  112.6 25.3 %bitcast_reduce_fusion = (f32[16,4,512]{2,0,1:T(8,128)S(1)}, f32[4,510,16,512]{3,1,2,0:T(8,128)}) fusion(bf16[16,512,256]{2,1,0:T(8,128)(2,1)} %all-gather.3.cloned.1.call-done, bf16[4,510,256,1]{2,0,1,3:T(4,128)(2,1)S(1)} %bitcast.99), kind=kOutput, calls=%fused_computation.2 | convolution fusion | flops 8589770752 | bytes 72216576 | tf_op jit(solution)/shard_map/brc,fpc->bfpr/dot_general | solution.py:27
  137.9 36.5 %fusion.2 = (f32[16,4,512]{2,0,1:T(8,128)S(1)}, f32[16,4,512]{2,0,1:T(8,128)S(1)}, f32[16,4,512]{2,0,1:T(8,128)S(1)}) fusion(f32[4,510,16,512]{3,1,2,0:T(8,128)} %get-tuple-element.18, f32[16,4,512]{2,0,1:T(8,128)S(1)} %get-tuple-element.17, f32[510]{0:T(512)S(1)} %get-tuple-element.22, f32[510]{0:T(512)S(1)} %get-tuple-element.21), kind=kLoop, calls=%fused_computation.6 | loop fusion | flops 116883456 | bytes 67375088 | tf_op jit(solution)/shard_map/reduce_sum | solution.py:35
  174.5 1.1 copy.79
  175.6 5.0 %all-to-all-start = ((f32[16,4,4,512]{3,2,1,0:T(4,128)}), f32[16,4,4,512]{3,2,1,0:T(4,128)S(1)}, u32[]{:S(2)}, u32[]{:S(2)}) async-start(f32[16,4,4,512]{3,2,1,0:T(4,128)} %copy.79), calls=%async_computation | async-start | bytes 1048576 | tf_op jit(solution)/shard_map/all_to_all | solution.py:41
  180.7 0.7 all_to_all.28
  181.4 13.4 %all-to-all-done = f32[16,4,4,512]{3,2,1,0:T(4,128)S(1)} async-done(((f32[16,4,4,512]{3,2,1,0:T(4,128)}), f32[16,4,4,512]{3,2,1,0:T(4,128)S(1)}, u32[]{:S(2)}, u32[]{:S(2)}) %all-to-all-start) | async-done | bytes 524320 | tf_op jit(solution)/shard_map/all_to_all | solution.py:41
  194.8 0.1 fusion.22
  194.9 0.1 div.112
  195.0 0.1 reduce_sum.106
  195.1 0.1 div.106
  195.2 0.1 reduce_sum.104
  195.3 0.6 pad_maximum_fusion.1
  (21 shorter events, 0.3 us)
Async XLA Ops:
  7.2 105.4 %all-gather.3.cloned.1.call-start = ((), (), s32[]{:S(2)}) async-start(), calls=%async_computation.3 | async-start | bytes 4456448 | tf_op jit(solution)/shard_map/all_gather | solution.py:20
  9.3 27.1 %all-to-all-start.1 = ((s32[2,64,2]{2,0,1:T(2,128)}), s32[2,64,2]{2,0,1:T(2,128)S(1)}, u32[]{:S(2)}, u32[]{:S(2)}) async-start(s32[2,64,2]{2,0,1:T(2,128)} %copy.87), calls=%async_computation.1 | async-start | bytes 131072 | tf_op jit(solution)/shard_map/all_to_all | solution.py:60
  36.8 75.8 %copy-start = (bf16[4,510,256]{2,0,1:T(4,128)(2,1)S(1)}, bf16[4,510,256]{2,0,1:T(4,128)(2,1)}, u32[]{:S(2)}) copy-start(bf16[4,510,256]{2,0,1:T(4,128)(2,1)} %param.8) | copy-start | bytes 3133444
  42.1 133.5 %all-to-all-start.2 = ((f32[2,4,32]{1,0,2:T(2,128)}), f32[2,4,32]{1,0,2:T(2,128)S(1)}, u32[]{:S(2)}, u32[]{:S(2)}) async-start(f32[2,4,32]{1,0,2:T(2,128)} %copy.93), calls=%async_computation.2 | async-start | bytes 65536 | tf_op jit(solution)/shard_map/all_to_all | solution.py:92
  175.6 19.1 %all-to-all-start = ((f32[16,4,4,512]{3,2,1,0:T(4,128)}), f32[16,4,4,512]{3,2,1,0:T(4,128)S(1)}, u32[]{:S(2)}, u32[]{:S(2)}) async-start(f32[16,4,4,512]{3,2,1,0:T(4,128)} %copy.79), calls=%async_computation | async-start | bytes 1048576 | tf_op jit(solution)/shard_map/all_to_all | solution.py:41
Sparse Core Ops, SparseCore 0:
  10.6 101.9 all-gather.2

commit v2 on v1

v2 whole, which is shorter than its diff:
```python
import functools
import math

import jax
import jax.numpy as jnp
from jax import lax
from jax.experimental import pallas as pl
from jax.experimental.pallas import tpu as pltpu
from jax.sharding import PartitionSpec as P

GH = 68
GW = 120
TILE = 8
SPREAD = 32.0
NT = (((1,), (1,)), ((), ()))
RING = 8
PEERS = 16
BLOCK = 15
SCALE = math.log2(math.e) / 16.0


def coarse_group(query, feat, first_block):
    rows = query.shape[0]
    sub = lax.broadcasted_iota(jnp.int32, (8, rows), 0)
    odd = (sub >= 4).astype(jnp.float32)
    top = jnp.full((8, rows), -jnp.inf, jnp.float32)
    total = jnp.zeros((8, rows), jnp.float32)
    row_sum = total
    col_sum = total
    for k in range(9):
        runs = 2 if k < 8 else 1
        size = 240 if k < 8 else 128
        scores = lax.dot_general(
            feat[k * 240 : k * 240 + size, :], query, NT, preferred_element_type=jnp.float32
        )
        scores = scores[: runs * BLOCK * 8].reshape(runs * BLOCK, 8, rows)
        new_top = jnp.maximum(top, jnp.max(scores, axis=0))
        keep = jnp.exp2((top - new_top) * SCALE)
        top = new_top
        total = total * keep
        row_sum = row_sum * keep
        col_sum = col_sum * keep
        for h in range(runs):
            run = moment = None
            for a in range(BLOCK - 1, -1, -1):
                weight = jnp.exp2((scores[h * BLOCK + a] - top) * SCALE)
                run = weight if run is None else run + weight
                if a > 0:
                    moment = run if moment is None else moment + run
            block = first_block + (2 * k + h)
            row = (block // 4).astype(jnp.float32) - (GH - 1) / 2.0
            col = ((block % 4) * 30).astype(jnp.float32) - (GW - 1) / 2.0
            total = total + run
            row_sum = row_sum + run * row
            col_sum = col_sum + (run * (col + odd) + 2.0 * moment)
    both = jnp.maximum(top, pltpu.roll(top, 4, 0))
    keep = jnp.exp2((top - both) * SCALE)
    total = total * keep
    row_sum = row_sum * keep
    col_sum = col_sum * keep
    total = total + pltpu.roll(total, 4, 0)
    row_sum = row_sum + pltpu.roll(row_sum, 4, 0)
    col_sum = col_sum + pltpu.roll(col_sum, 4, 0)
    low = sub < 4
    return jnp.where(low, both, total), jnp.where(low, row_sum, col_sum)


def coarse_combine(stats, out):
    rows = stats.shape[-1]
    low = lax.broadcasted_iota(jnp.int32, (8, rows), 0) < 4
    tops = []
    for i in range(PEERS):
        first = stats[i, 0]
        tops.append(jnp.where(low, first, pltpu.roll(first, 4, 0)))
    top = functools.reduce(jnp.maximum, tops)
    total = jnp.zeros((8, rows), jnp.float32)
    sums = total
    for i in range(PEERS):
        factor = jnp.exp2((tops[i] - top) * SCALE)
        total = total + stats[i, 0] * factor
        sums = sums + stats[i, 1] * factor
    total = jnp.where(low, pltpu.roll(total, 4, 0), total)
    mean = sums / total
    head = lax.broadcasted_iota(jnp.int32, (rows, 128), 0) // 16
    track = lax.broadcasted_iota(jnp.int32, (rows, 128), 1)
    pick = (head == track).astype(jnp.float32)
    mean = jnp.dot(
        mean, pick, preferred_element_type=jnp.float32, precision=lax.Precision.HIGHEST
    ) * (1.0 / 16.0)
    out[0] = mean[0:4, 0:32] * (1.0 / (GH / 4.0))
    out[1] = mean[4:8, 0:32] * (1.0 / (GW / 4.0))


def fine_frames(region, blk, frame_block, lists, valid, gathered, tiles, words, place, fscore, reply):
    lane = lax.broadcasted_iota(jnp.int32, (32, 128), 1)
    step = lax.broadcasted_iota(jnp.int32, (32, 128), 0)
    cell = blk * region + 2 * step + (lane >> 6)
    row = (cell * 34953) >> 22
    col = cell - row * GW
    place[0] = (row * TILE + ((lane & 63) >> 3)).astype(jnp.float32)
    place[1] = (col * TILE + (lane & 7)).astype(jnp.float32)
    words[...] = jnp.zeros_like(words)
    ids = lists[...]
    live = valid[...] > 0
    for k in range(4):
        bits = jnp.where(
            jnp.logical_and((ids >> 4) == k, live), jnp.left_shift(1, ids & 15), 0
        ).astype(jnp.float32)
        words[k * 4 : k * 4 + 4, 0:16] = jnp.sum(bits, axis=1)
    by_owner = jnp.transpose(words[...])[0:16]
    by_track = jnp.concatenate([by_owner, by_owner], axis=0)
    descs = jnp.concatenate([gathered[:, 0, :], gathered[:, 1, :]], axis=0).astype(jnp.bfloat16)
    track_row = jnp.concatenate([gathered[:, 2, :], gathered[:, 3, :]], axis=0)
    track_col = jnp.concatenate([gathered[:, 4, :], gathered[:, 5, :]], axis=0)
    right_half = lane >= 64

    def column(array, index):
        picked = jnp.sum(jnp.where(lane == index, array, 0.0), axis=1, keepdims=True)
        return jnp.broadcast_to(picked, (32, 128))

    def frame(w, results):
        at = frame_block * 4 + w
        here_row = column(track_row, at)
        here_col = column(track_col, at)
        masks = []
        for k in range(4):
            word = column(by_track, k * 4 + w).astype(jnp.int32)
            masks.append(jnp.where(right_half, word >> 1, word))
        top = jnp.full((32, 128), -1e30, jnp.float32)
        for q in range(8):
            scores = lax.dot_general(
                descs, tiles[w, q * 512 : q * 512 + 512, :], NT, preferred_element_type=jnp.float32
            ) * (1.0 / math.sqrt(128))
            for h in range(4):
                j = q * 4 + h
                away_row = place[0, j : j + 1, :] - here_row
                away_col = place[1, j : j + 1, :] - here_col
                score = scores[:, h * 128 : h * 128 + 128] - (
                    away_row * away_row + away_col * away_col
                ) * (0.5 / (SPREAD * SPREAD))
                listed = (masks[j // 8] & (1 << (2 * j % 16))) != 0
                score = jnp.where(listed, score, -1e30)
                fscore[j] = score
                top = jnp.maximum(top, score)
        top = jnp.broadcast_to(jnp.max(top, axis=1, keepdims=True), (32, 128))
        total = jnp.zeros((32, 128), jnp.float32)
        row_sum = total
        col_sum = total
        for j in range(32):
            weight = jnp.exp(fscore[j] - top)
            total = total + weight
            row_sum = row_sum + weight * (place[0, j : j + 1, :] - here_row)
            col_sum = col_sum + weight * (place[1, j : j + 1, :] - here_col)
        total = jnp.sum(total, axis=1, keepdims=True)
        row_out = jnp.sum(row_sum, axis=1, keepdims=True) / total * (1.0 / SPREAD)
        col_out = jnp.sum(col_sum, axis=1, keepdims=True) / total * (1.0 / SPREAD)
        here = lane == at
        return (
            jnp.where(here, row_out, results[0]),
            jnp.where(here, col_out, results[1]),
        )

    zeros = jnp.zeros((32, 128), jnp.float32)
    rows, cols = lax.fori_loop(0, 4, frame, (zeros, zeros))
    reply[...] = jnp.zeros_like(reply)
    reply[:, 0, :] = rows[0:16]
    reply[:, 1, :] = rows[16:32]
    reply[:, 2, :] = cols[0:16]
    reply[:, 3, :] = cols[16:32]


def kernel(
    q_in, f_in, tiles_in, desc_in, pos_in, lists, valid,
    coarse_out, fine_out,
    queries, feat, tiles, stats_out, stats_in, note, gathered, reply, answers, words, place, fscore,
    local_sem, y_sem, z_send, z_recv, c_send, c_recv, s_send, s_recv, n_send, n_recv, a_send, a_recv,
):
    blk = lax.axis_index("blk")
    frames = lax.axis_index("frames")
    z = blk % RING
    yh = blk // RING
    core = frames % 2
    half = pl.multiple_of(core * 256, 256)
    cross = {"blk": (1 - yh) * RING + z, "frames": frames + 2 - 4 * ((frames // 2) % 2)}
    sibling = {"blk": blk, "frames": frames + 1 - 2 * core}

    def ring(k):
        return (z + (RING + k)) % RING

    locals_ = [
        pltpu.make_async_copy(q_in, queries.at[z, yh], local_sem.at[0]),
        pltpu.make_async_copy(f_in, feat, local_sem.at[1]),
        pltpu.make_async_copy(tiles_in, tiles, local_sem.at[2]),
    ]
    for c in locals_:
        c.start()

    barrier = pltpu.get_barrier_semaphore()

    def greet(i, _):
        pl.semaphore_signal(barrier, inc=1, device_id={"blk": (blk + i) % PEERS, "frames": frames})
        pl.semaphore_signal(barrier, inc=1, device_id={"blk": blk, "frames": (frames + i) % PEERS})
        return 0

    lax.fori_loop(1, PEERS, greet, 0)
    pl.semaphore_signal(barrier, inc=1, device_id=cross)

    note[...] = jnp.zeros_like(note)
    note[0:2, :] = desc_in[...].astype(jnp.float32)
    note[2:4, 0:64] = pos_in[0].astype(jnp.float32)
    note[4:6, 0:64] = pos_in[1].astype(jnp.float32)
    pl.semaphore_wait(barrier, 2 * (PEERS - 1) + 1)

    def remote(src, dst, send, recv, to):
        return pltpu.make_async_remote_copy(
            src_ref=src, dst_ref=dst, send_sem=send, recv_sem=recv,
            device_id=to, device_id_type=pl.DeviceIdType.MESH,
        )

    own = q_in.at[pl.ds(half, 256)]
    y_copy = remote(own, queries.at[z, yh, pl.ds(half, 256)], y_sem.at[0], y_sem.at[1], cross)

    def z_copy(way, stage):
        to = {"blk": yh * RING + ring(1 - 2 * way), "frames": frames}
        sems = (z_send.at[way, stage], z_recv.at[way, stage])
        if stage == 0:
            return remote(own, queries.at[z, yh, pl.ds(half, 256)], *sems, to)
        if stage == 1:
            ref = queries.at[z, 1 - yh, pl.ds(half, 256)]
        elif stage < 4:
            ref = queries.at[ring((stage - 1) * (2 * way - 1)), :, pl.ds(half, 256)]
        else:
            ref = queries.at[
                ring((stage - 1) * (2 * way - 1)), :, pl.ds(pl.multiple_of(half + 128 * way, 128), 128)
            ]
        return remote(ref, ref, *sems, to)

    def c_copy(k):
        if k == 0:
            ref = queries.at[z, 1 - yh, pl.ds(half, 256)]
        else:
            ref = queries.at[ring({1: -1, 2: -2, 3: -3, 4: 1, 5: 2, 6: 3, 7: -4}[k]), :, pl.ds(half, 256)]
        return remote(ref, ref, c_send.at[k], c_recv.at[k], sibling)

    def note_copy(i):
        return remote(
            note, gathered.at[frames], n_send.at[i], n_recv.at[i],
            {"blk": blk, "frames": (frames + i) % PEERS},
        )

    def answer_copy(i):
        to = (frames + i) % PEERS
        return remote(
            reply.at[to], answers.at[i], a_send.at[i], a_recv.at[i], {"blk": blk, "frames": to}
        )

    def group_of(i):
        j = i - 2
        away = j // 4 + 1
        left = (j % 4) // 2
        shift = jnp.where(i < 2, 0, jnp.where(left == 1, away, -away))
        return (z + RING + shift) % RING, (yh + i) % 2

    def stat_copy(i):
        gz, gy = group_of(i)
        return remote(
            stats_out.at[i], stats_in.at[i], s_send.at[i], s_recv.at[i],
            {"blk": gy * RING + gz, "frames": frames},
        )

    y_copy.start()
    z_copy(0, 0).start()
    z_copy(1, 0).start()

    def start_notes(i, _):
        note_copy(i).start()
        return 0

    lax.fori_loop(1, PEERS, start_notes, 0)
    gathered[frames] = note[...]
    locals_[0].wait()
    locals_[1].wait()

    def fine_stage():
        locals_[2].wait()

        def wait_notes(i, _):
            note_copy(i).wait_recv()
            return 0

        lax.fori_loop(1, PEERS, wait_notes, 0)
        fine_frames(
            510, blk, frames, lists, valid, gathered, tiles, words, place, fscore, reply
        )
        answers[0] = reply[frames]

        def start_answers(i, _):
            answer_copy(i).start()
            return 0

        lax.fori_loop(1, PEERS, start_answers, 0)

    def arrive(stage):
        for way in range(2):
            if stage == 1:
                z_copy(way, 0).wait_recv()
                z_copy(way, 1).wait_recv()
            else:
                z_copy(way, stage).wait_recv()
            if stage < 4:
                z_copy(way, stage + 1).start()
        if stage < 4:
            c_copy(stage).start()
            c_copy(stage + 3).start()
        else:
            c_copy(7).start()

    def group_step(i, _):
        @pl.when(i == 1)
        def _():
            y_copy.wait_recv()
            z_copy(0, 1).start()
            z_copy(1, 1).start()
            c_copy(0).start()
            fine_stage()
            c_copy(0).wait_recv()

        @pl.when(i == 2)
        def _():
            arrive(1)
            c_copy(1).wait_recv()
            c_copy(4).wait_recv()

        @pl.when(i == 5)
        def _():
            arrive(2)

        @pl.when(i == 6)
        def _():
            c_copy(2).wait_recv()
            c_copy(5).wait_recv()

        @pl.when(i == 9)
        def _():
            arrive(3)

        @pl.when(i == 10)
        def _():
            c_copy(3).wait_recv()
            c_copy(6).wait_recv()

        @pl.when(i == 12)
        def _():
            arrive(4)

        @pl.when(i == 14)
        def _():
            c_copy(7).wait_recv()

        gz, gy = group_of(i)
        first, second = coarse_group(queries[gz, gy], feat, blk * 17)

        @pl.when(i == 0)
        def _():
            stats_in[0, 0] = first
            stats_in[0, 1] = second

        @pl.when(i > 0)
        def _():
            stats_out[i, 0] = first
            stats_out[i, 1] = second
            stat_copy(i).start()

        return 0

    lax.fori_loop(0, PEERS, group_step, 0)

    def wait_stats(i, _):
        stat_copy(i).wait_recv()
        answer_copy(i).wait_recv()
        return 0

    lax.fori_loop(1, PEERS, wait_stats, 0)
    coarse_combine(stats_in, coarse_out)
    answer = jnp.sum(answers[...], axis=0)
    fine_out[0] = answer[0:2, 0:64]
    fine_out[1] = answer[2:4, 0:64]

    def wait_sends(i, _):
        stat_copy(i).wait_send()
        answer_copy(i).wait_send()
        note_copy(i).wait_send()
        return 0

    lax.fori_loop(1, PEERS, wait_sends, 0)
    y_copy.wait_send()
    for way in range(2):
        for stage in range(5):
            z_copy(way, stage).wait_send()
    for k in range(8):
        c_copy(k).wait_send()


def body(coarse_query, coarse_feat, fine_query, fine_tiles, track_pos, tile_list, tile_valid):
    track_group, heads, channels = coarse_query.shape
    frames_here, region, _ = coarse_feat.shape
    queries = coarse_query.reshape(track_group * heads, channels)
    feat = jnp.transpose(coarse_feat, (1, 0, 2)).reshape(region * frames_here, channels)
    feat = jnp.pad(feat, ((0, 8), (0, 0)))
    tiles = fine_tiles.reshape(frames_here, -1, fine_tiles.shape[-1])
    pos = jnp.transpose(track_pos, (0, 2, 1))
    lists = jnp.transpose(tile_list[:, 0], (0, 2, 1))
    valid = jnp.transpose(tile_valid[:, 0], (0, 2, 1))
    f32 = jnp.float32
    vmem = pl.BlockSpec(memory_space=pltpu.VMEM)
    far = pl.BlockSpec(memory_space=pl.ANY)
    dma = pltpu.SemaphoreType.DMA
    rows = queries.shape[0]
    coarse_pos, offset = pl.pallas_call(
        kernel,
        out_shape=(
            jax.ShapeDtypeStruct((2, 4, 32), f32),
            jax.ShapeDtypeStruct((2, 2, 64), f32),
        ),
        in_specs=[far, far, far, vmem, vmem, vmem, vmem],
        out_specs=(vmem, vmem),
        scratch_shapes=[
            pltpu.VMEM((RING, 2, rows, channels), jnp.bfloat16),
            pltpu.VMEM(feat.shape, jnp.bfloat16),
            pltpu.VMEM(tiles.shape, jnp.bfloat16),
            pltpu.VMEM((PEERS, 2, 8, rows), f32),
            pltpu.VMEM((PEERS, 2, 8, rows), f32),
            pltpu.VMEM((8, 128), f32),
            pltpu.VMEM((PEERS, 8, 128), f32),
            pltpu.VMEM((PEERS, 8, 128), f32),
            pltpu.VMEM((PEERS, 8, 128), f32),
            pltpu.VMEM((128, 128), f32),
            pltpu.VMEM((2, 32, 128), f32),
            pltpu.VMEM((32, 32, 128), f32),
            dma((3,)),
            dma((2,)),
            dma((2, 5)),
            dma((2, 5)),
            dma((8,)),
            dma((8,)),
            dma((PEERS,)),
            dma((PEERS,)),
            dma((PEERS,)),
            dma((PEERS,)),
            dma((PEERS,)),
            dma((PEERS,)),
        ],
        compiler_params=pltpu.CompilerParams(
            collective_id=0, has_side_effects=True, vmem_limit_bytes=56 * 2**20
        ),
        cost_estimate=pl.CostEstimate(
            flops=2 * 8192 * 2048 * 256, bytes_accessed=6 * 10**6, transcendentals=8192 * 2048
        ),
    )(queries, feat, tiles, fine_query, pos, lists, valid)
    return coarse_pos, jnp.transpose(offset, (0, 2, 1))


def solution(mesh):
    return jax.shard_map(
        body,
        mesh=mesh,
        in_specs=(
            P("blk", None, None),
            P("frames", "blk", None),
            P(("blk", "frames"), None),
            P("frames", "blk", None, None),
            P(None, None, ("blk", "frames")),
            P("frames", "blk", None, None),
            P("frames", "blk", None, None),
        ),
        out_specs=(P(None, "frames", "blk"), P(None, None, ("blk", "frames"))),
        check_vma=False,
    )
```

time: 203 us -> 63.5 us (0.31)
  waiting for transfers between devices: 76.4 us -> 0 us
  Pallas kernels: 0 us -> 56.4 us
  other arithmetic: 38.6 us -> 0 us
  matrix products: 30 us -> 0 us
  starting transfers between devices: 18.9 us -> 0 us
  blocking collectives: 15.4 us -> 0 us
  between operations: 14.2 us -> 0.65 us
  local copies, waits for them, and re-layouts: 9.39 us -> 5.28 us
    all_gather x1 -> x0, waiting for transfers between devices: 62.3 us -> none  [coarse(): lax.all_gather(coarse_query.reshape(track_group * heads, channels), 'blk'...]
    pallas_call x0 -> x1, Pallas kernels: none -> 56.4 us  [body(): pl.pallas_call(kernel, out_shape=(jax.ShapeDtypeStruct((2, 4, 32), f32),...]
    reduce_sum x4 -> x0, other arithmetic: 36.8 us -> none  [the longest x1 36.5 us: coarse(): jnp.sum(weights, axis=2)]
    dot_general x1 -> x0, matrix products: 25.3 us -> none  [coarse(): jnp.einsum('brc,fpc->bfpr', queries, coarse_feat, preferred_element_type=...]
    all_to_all x3 -> x0, starting transfers between devices: 18.8 us -> none  [the longest x1 8.1 us: fine(): lax.all_to_all(out, 'frames', split_axis=2, concat_axis=1, tiled=True)]
    all_gather x1 -> x0, blocking collectives: 15.4 us -> none  [fine(): descs = lax.all_gather(fine_query, 'frames', axis=0, tiled=True)]
    all_to_all x3 -> x0, waiting for transfers between devices: 13.4 us -> none  [the longest x1 13.4 us: coarse(): lax.all_to_all(stats, 'blk', split_axis=0, concat_axis=0, tiled=True)]
    sub x1 -> x0, matrix products: 4.63 us -> none  [fine(): weights = jnp.exp(scores - jnp.max(scores, axis=2, keepdims=True))]
  transfers between devices with their start and end apart: 4 -> 0, of which waited for: 2 -> 0; matrix products, arithmetic and copies ran while one was open for 38% -> 0% of each run, Pallas kernels for 0% -> 0%
where the time goes in v2:
time: 63.5 us; the launch traced here: 62.3 us
  Pallas kernels  56.4 us (89%)
  local copies, waits for them, and re-layouts  5.28 us (8%)
  between operations  0.65 us (1%)
    pallas_call x1, Pallas kernels, body(): pl.pallas_call(kernel, out_shape=(jax.ShapeDtypeStruct((2, 4, 32), f32),...  56.4 us
    unnamed x2, local copies, waits for them, and re-layouts  2.5 us
    reshape x1, local copies, waits for them, and re-layouts, body(): jnp.transpose(coarse_feat, (1, 0, 2))  1.72 us

profile of v2, /device:TPU:14, one launch (start us, length us, event | category | flops | bytes accessed | tf_op | source)
XLA Modules:
  0.0 62.3 jit_solution(4857809057402989713)
XLA Ops:
  0.6 1.7 %reshape.14 = bf16[2040,256]{1,0:T(8,128)(2,1)S(1)} reshape(bf16[510,4,256]{2,1,0:T(4,128)(2,1)} %bitcast.11) | data formatting | bytes 2088960 | tf_op jit(solution)/shard_map/reshape | solution.py:408
  2.4 1.1 %pad.4.f_in = bf16[2048,256]{1,0:T(8,128)(2,1)} pad(bf16[2040,256]{1,0:T(8,128)(2,1)S(1)} %reshape.14, bf16[]{:T(256)} %constant.2.clone.1), padding=0_8x0_0 | pad | bytes 2093058 | tf_op jit(solution)/shard_map/jit(_pad)/pad | solution.py:409
  3.4 56.4 %shard_map.86 = (f32[2,4,32]{2,1,0:T(4,128)}, f32[2,2,64]{2,1,0:T(2,128)}) custom-call(bf16[512,256]{1,0:T(8,128)(2,1)} %bitcast.14, bf16[2048,256]{1,0:T(8,128)(2,1)} %pad.4.f_in, bf16[4,4096,128]{2,1,0:T(8,128)(2,1)} %bitcast.13, bf16[2,128]{1,0:T(2,128)(2,1)} %desc_in.1, s32[2,2,64]{2,1,0:T(2,128)} %bitcast.17, s32[4,8,16]{2,1,0:T(8,128)} %bitcast.15, ...), custom_call_target="tpu_custom_call" | custom-call | flops 8589934592 | bytes 6000000 | tf_op jit(solution)/shard_map/pallas_call | solution.py:419
  59.8 1.3 %copy.11 = f32[2,4,32]{2,1,0:T(4,128)} copy(f32[2,4,32]{2,1,0:T(4,128)} %get-tuple-element.8) | data formatting | bytes 2048
  61.1 1.2 %copy.12 = f32[2,64,2]{1,2,0:T(2,128)} copy(f32[2,64,2]{1,2,0:T(2,128)} %bitcast.12) | data formatting | bytes 2048

commit v3 on v2

--- a/solution.py
+++ b/solution.py
@@ -16,6 +16,25 @@
 RING = 8
 PEERS = 16
 BLOCK = 15
+ORDER = (
+    (0, 0), (1, 0), (0, -1), (0, 1), (0, -2), (0, 2), (1, -1), (1, 1),
+    (0, -3), (0, 3), (1, -2), (1, 2), (0, 4), (1, -3), (1, 3), (1, 4),
+)
+EVENTS = {
+    1: (
+        ("near", 1, 0), ("near", 1, 1), ("across", 0), ("fine",), ("near", 2, 0), ("near", 2, 1), ("ready", 1, 0),
+    ),
+    2: (("ready", 0, 1),),
+    3: (("near", 3, 0),),
+    4: (("near", 3, 1), ("across", 1), ("ready", 0, 2)),
+    6: (("ready", 1, 1),),
+    7: (("near", 4, 0), ("across", 2)),
+    8: (("ready", 0, 3),),
+    10: (("across", 3), ("ready", 1, 2)),
+    12: (("ready", 0, 4), ("across", 4)),
+    13: (("ready", 1, 3),),
+    15: (("ready", 1, 4),),
+}
 SCALE = math.log2(math.e) / 16.0
 
 
@@ -173,19 +192,19 @@
     q_in, f_in, tiles_in, desc_in, pos_in, lists, valid,
     coarse_out, fine_out,
     queries, feat, tiles, stats_out, stats_in, note, gathered, reply, answers, words, place, fscore,
-    local_sem, y_sem, z_send, z_recv, c_send, c_recv, s_send, s_recv, n_send, n_recv, a_send, a_recv,
+    local_sem, near_send, y_recv, z_recv, c_recv, far_send, far_recv,
 ):
     blk = lax.axis_index("blk")
     frames = lax.axis_index("frames")
-    z = blk % RING
-    yh = blk // RING
-    core = frames % 2
+    z = blk & (RING - 1)
+    yh = blk >> 3
+    core = frames & 1
     half = pl.multiple_of(core * 256, 256)
-    cross = {"blk": (1 - yh) * RING + z, "frames": frames + 2 - 4 * ((frames // 2) % 2)}
+    cross = {"blk": (1 - yh) * RING + z, "frames": frames + 2 - 2 * (frames & 2)}
     sibling = {"blk": blk, "frames": frames + 1 - 2 * core}
 
     def ring(k):
-        return (z + (RING + k)) % RING
+        return (z + (RING + k)) & (RING - 1)
 
     locals_ = [
         pltpu.make_async_copy(q_in, queries.at[z, yh], local_sem.at[0]),
@@ -198,8 +217,8 @@
     barrier = pltpu.get_barrier_semaphore()
 
     def greet(i, _):
-        pl.semaphore_signal(barrier, inc=1, device_id={"blk": (blk + i) % PEERS, "frames": frames})
-        pl.semaphore_signal(barrier, inc=1, device_id={"blk": blk, "frames": (frames + i) % PEERS})
+        pl.semaphore_signal(barrier, inc=1, device_id={"blk": (blk + i) & (PEERS - 1), "frames": frames})
+        pl.semaphore_signal(barrier, inc=1, device_id={"blk": blk, "frames": (frames + i) & (PEERS - 1)})
         return 0
 
     lax.fori_loop(1, PEERS, greet, 0)
@@ -209,7 +228,6 @@
     note[0:2, :] = desc_in[...].astype(jnp.float32)
     note[2:4, 0:64] = pos_in[0].astype(jnp.float32)
     note[4:6, 0:64] = pos_in[1].astype(jnp.float32)
-    pl.semaphore_wait(barrier, 2 * (PEERS - 1) + 1)
 
     def remote(src, dst, send, recv, to):
         return pltpu.make_async_remote_copy(
@@ -218,77 +236,87 @@
         )
 
     own = q_in.at[pl.ds(half, 256)]
-    y_copy = remote(own, queries.at[z, yh, pl.ds(half, 256)], y_sem.at[0], y_sem.at[1], cross)
-
-    def z_copy(way, stage):
+    def part(chain, shift, start, size):
+        return queries.at[ring(shift), yh if chain == 0 else 1 - yh, pl.ds(start, size)]
+
+    def rows_of(chunk):
+        return pl.multiple_of(half + 128 * chunk, 128)
+
+    def z_copy(way, stage, chunk):
         to = {"blk": yh * RING + ring(1 - 2 * way), "frames": frames}
-        sems = (z_send.at[way, stage], z_recv.at[way, stage])
+        at = 2 * (stage - 1) + chunk
+        dst = part(0, (stage - 1) * (2 * way - 1), rows_of(chunk), 128)
+        src = q_in.at[pl.ds(rows_of(chunk), 128)] if stage == 1 else dst
+        return remote(src, dst, near_send.at[0], z_recv.at[way, at], to)
+
+    def y_copy(way, stage, chunk):
         if stage == 0:
-            return remote(own, queries.at[z, yh, pl.ds(half, 256)], *sems, to)
-        if stage == 1:
-            ref = queries.at[z, 1 - yh, pl.ds(half, 256)]
+            return remote(own, part(0, 0, half, 256), near_send.at[1], y_recv.at[0, 8], cross)
+        at = 2 * (stage - 1) + chunk
+        ref = part(0, stage * (2 * way - 1), rows_of(chunk), 128)
+        return remote(ref, ref, near_send.at[1], y_recv.at[way, at], cross)
+
+    def c_copy(chain, way, stage):
+        if stage == 0:
+            k = 0
         elif stage < 4:
-            ref = queries.at[ring((stage - 1) * (2 * way - 1)), :, pl.ds(half, 256)]
+            k = 1 + chain * 6 + way * 3 + stage - 1
         else:
-            ref = queries.at[
-                ring((stage - 1) * (2 * way - 1)), :, pl.ds(pl.multiple_of(half + 128 * way, 128), 128)
-            ]
-        return remote(ref, ref, *sems, to)
-
-    def c_copy(k):
-        if k == 0:
-            ref = queries.at[z, 1 - yh, pl.ds(half, 256)]
-        else:
-            ref = queries.at[ring({1: -1, 2: -2, 3: -3, 4: 1, 5: 2, 6: 3, 7: -4}[k]), :, pl.ds(half, 256)]
-        return remote(ref, ref, c_send.at[k], c_recv.at[k], sibling)
+            k = 13 + chain
+        ref = part(chain, stage * (2 * way - 1), half, 256)
+        return remote(ref, ref, near_send.at[2], c_recv.at[k], sibling)
+
+    Z_PARTS = [(w, d, c) for w in range(2) for d in range(1, 5) for c in range(2) if d < 4 or c == w]
 
     def note_copy(i):
         return remote(
-            note, gathered.at[frames], n_send.at[i], n_recv.at[i],
-            {"blk": blk, "frames": (frames + i) % PEERS},
+            note, gathered.at[frames], far_send.at[0], far_recv.at[0],
+            {"blk": blk, "frames": (frames + i) & (PEERS - 1)},
         )
 
     def answer_copy(i):
-        to = (frames + i) % PEERS
+        to = (frames + i) & (PEERS - 1)
         return remote(
-            reply.at[to], answers.at[i], a_send.at[i], a_recv.at[i], {"blk": blk, "frames": to}
+            reply.at[to], answers.at[i], far_send.at[1], far_recv.at[1], {"blk": blk, "frames": to}
         )
 
     def group_of(i):
-        j = i - 2
-        away = j // 4 + 1
-        left = (j % 4) // 2
-        shift = jnp.where(i < 2, 0, jnp.where(left == 1, away, -away))
-        return (z + RING + shift) % RING, (yh + i) % 2
+        chain = away = i * 0
+        for at, (n, k) in enumerate(ORDER):
+            chain = jnp.where(i == at, n, chain)
+            away = jnp.where(i == at, k, away)
+        return (z + RING + away) & (RING - 1), (yh + chain) & 1
 
     def stat_copy(i):
         gz, gy = group_of(i)
         return remote(
-            stats_out.at[i], stats_in.at[i], s_send.at[i], s_recv.at[i],
+            stats_out.at[i], stats_in.at[i], far_send.at[2], far_recv.at[2],
             {"blk": gy * RING + gz, "frames": frames},
         )
 
-    y_copy.start()
-    z_copy(0, 0).start()
-    z_copy(1, 0).start()
+    def wait_all(ref, sem):
+        pltpu.make_async_copy(ref, ref, sem).wait()
 
     def start_notes(i, _):
         note_copy(i).start()
         return 0
 
-    lax.fori_loop(1, PEERS, start_notes, 0)
-    gathered[frames] = note[...]
+    def enter():
+        pl.semaphore_wait(barrier, 2 * (PEERS - 1) + 1)
+        for chunk in range(2):
+            z_copy(0, 1, chunk).start()
+            z_copy(1, 1, chunk).start()
+        y_copy(0, 0, 0).start()
+        lax.fori_loop(1, PEERS, start_notes, 0)
+        gathered[frames] = note[...]
+
     locals_[0].wait()
     locals_[1].wait()
 
     def fine_stage():
         locals_[2].wait()
 
-        def wait_notes(i, _):
-            note_copy(i).wait_recv()
-            return 0
-
-        lax.fori_loop(1, PEERS, wait_notes, 0)
+        wait_all(gathered.at[1:PEERS], far_recv.at[0])
         fine_frames(
             510, blk, frames, lists, valid, gathered, tiles, words, place, fscore, reply
         )
@@ -300,62 +328,47 @@
 
         lax.fori_loop(1, PEERS, start_answers, 0)
 
-    def arrive(stage):
+    def near(stage, chunk):
         for way in range(2):
-            if stage == 1:
-                z_copy(way, 0).wait_recv()
-                z_copy(way, 1).wait_recv()
-            else:
-                z_copy(way, stage).wait_recv()
-            if stage < 4:
-                z_copy(way, stage + 1).start()
+            if stage == 4:
+                chunk = way
+            z_copy(way, stage, chunk).wait_recv()
+            if stage < 3 or (stage == 3 and chunk == way):
+                z_copy(way, stage + 1, chunk).start()
+            y_copy(way, stage, chunk).start()
+        if stage == 4:
+            c_copy(0, 0, 4).start()
+        elif chunk == 1:
+            c_copy(0, 0, stage).start()
+            c_copy(0, 1, stage).start()
+
+    def across(stage):
+        if stage == 0:
+            y_copy(0, 0, 0).wait_recv()
+            c_copy(1, 0, 0).start()
+            return
+        for way, d, chunk in Z_PARTS:
+            if d == stage:
+                y_copy(way, d, chunk).wait_recv()
+        c_copy(1, 0, stage).start()
         if stage < 4:
-            c_copy(stage).start()
-            c_copy(stage + 3).start()
-        else:
-            c_copy(7).start()
+            c_copy(1, 1, stage).start()
+
+    def ready(chain, stage):
+        c_copy(chain, 0, stage).wait_recv()
+        if 0 < stage < 4:
+            c_copy(chain, 1, stage).wait_recv()
 
     def group_step(i, _):
-        @pl.when(i == 1)
+        @pl.when(i == 0)
         def _():
-            y_copy.wait_recv()
-            z_copy(0, 1).start()
-            z_copy(1, 1).start()
-            c_copy(0).start()
-            fine_stage()
-            c_copy(0).wait_recv()
-
-        @pl.when(i == 2)
-        def _():
-            arrive(1)
-            c_copy(1).wait_recv()
-            c_copy(4).wait_recv()
-
-        @pl.when(i == 5)
-        def _():
-            arrive(2)
-
-        @pl.when(i == 6)
-        def _():
-            c_copy(2).wait_recv()
-            c_copy(5).wait_recv()
-
-        @pl.when(i == 9)
-        def _():
-            arrive(3)
-
-        @pl.when(i == 10)
-        def _():
-            c_copy(3).wait_recv()
-            c_copy(6).wait_recv()
-
-        @pl.when(i == 12)
-        def _():
-            arrive(4)
-
-        @pl.when(i == 14)
-        def _():
-            c_copy(7).wait_recv()
+            enter()
+
+        for when, events in EVENTS.items():
+            @pl.when(i == when)
+            def _(events=events):
+                for event, *at in events:
+                    {"near": near, "across": across, "ready": ready, "fine": fine_stage}[event](*at)
 
         gz, gy = group_of(i)
         first, second = coarse_group(queries[gz, gy], feat, blk * 17)
@@ -375,30 +388,19 @@
 
     lax.fori_loop(0, PEERS, group_step, 0)
 
-    def wait_stats(i, _):
-        stat_copy(i).wait_recv()
-        answer_copy(i).wait_recv()
-        return 0
-
-    lax.fori_loop(1, PEERS, wait_stats, 0)
+    wait_all(answers.at[1:PEERS], far_recv.at[1])
+    wait_all(stats_in.at[1:PEERS], far_recv.at[2])
     coarse_combine(stats_in, coarse_out)
     answer = jnp.sum(answers[...], axis=0)
     fine_out[0] = answer[0:2, 0:64]
     fine_out[1] = answer[2:4, 0:64]
 
-    def wait_sends(i, _):
-        stat_copy(i).wait_send()
-        answer_copy(i).wait_send()
-        note_copy(i).wait_send()
-        return 0
-
-    lax.fori_loop(1, PEERS, wait_sends, 0)
-    y_copy.wait_send()
-    for way in range(2):
-        for stage in range(5):
-            z_copy(way, stage).wait_send()
-    for k in range(8):
-        c_copy(k).wait_send()
+    wait_all(gathered.at[1:PEERS], far_send.at[0])
+    wait_all(answers.at[1:PEERS], far_send.at[1])
+    wait_all(stats_in.at[1:PEERS], far_send.at[2])
+    wait_all(queries.at[0:7, 0, 0:256], near_send.at[0])
+    wait_all(queries.at[:, 0, 0:256], near_send.at[1])
+    wait_all(queries.at[:, 0, 0:480], near_send.at[2])
 
 
 def body(coarse_query, coarse_feat, fine_query, fine_tiles, track_pos, tile_list, tile_valid):
@@ -438,17 +440,12 @@
             pltpu.VMEM((2, 32, 128), f32),
             pltpu.VMEM((32, 32, 128), f32),
             dma((3,)),
-            dma((2,)),
-            dma((2, 5)),
-            dma((2, 5)),
-            dma((8,)),
-            dma((8,)),
-            dma((PEERS,)),
-            dma((PEERS,)),
-            dma((PEERS,)),
-            dma((PEERS,)),
-            dma((PEERS,)),
-            dma((PEERS,)),
+            dma((3,)),
+            dma((2, 9)),
+            dma((2, 8)),
+            dma((15,)),
+            dma((3,)),
+            dma((3,)),
         ],
         compiler_params=pltpu.CompilerParams(
             collective_id=0, has_side_effects=True, vmem_limit_bytes=56 * 2**20

time: 63.5 us -> 58.2 us (0.917); the launches traced: 62.3 us -> 57.9 us
  Pallas kernels: 56.4 us -> 52 us
    pallas_call x1, Pallas kernels: 56.4 us -> 52 us  [body(): pl.pallas_call(kernel, out_shape=(jax.ShapeDtypeStruct((2, 4, 32), f32),...]
where the time goes in v3:
time: 58.2 us; the launch traced here: 57.9 us
  Pallas kernels  52 us (89%)
  local copies, waits for them, and re-layouts  5.28 us (9%)
  between operations  0.65 us (1%)
    pallas_call x1, Pallas kernels, body(): pl.pallas_call(kernel, out_shape=(jax.ShapeDtypeStruct((2, 4, 32), f32),...  52 us
    unnamed x2, local copies, waits for them, and re-layouts  2.5 us
    reshape x1, local copies, waits for them, and re-layouts, body(): jnp.transpose(coarse_feat, (1, 0, 2))  1.72 us

profile of v3, /device:TPU:14, one launch (start us, length us, event | category | flops | bytes accessed | tf_op | source)
XLA Modules:
  0.0 57.9 jit_solution(14237659893880337238)
XLA Ops:
  0.6 1.7 %reshape.14 = bf16[2040,256]{1,0:T(8,128)(2,1)S(1)} reshape(bf16[510,4,256]{2,1,0:T(4,128)(2,1)} %bitcast.11) | data formatting | bytes 2088960 | tf_op jit(solution)/shard_map/reshape | solution.py:410
  2.4 1.1 %pad.4.f_in = bf16[2048,256]{1,0:T(8,128)(2,1)} pad(bf16[2040,256]{1,0:T(8,128)(2,1)S(1)} %reshape.14, bf16[]{:T(256)} %constant.2.clone.1), padding=0_8x0_0 | pad | bytes 2093058 | tf_op jit(solution)/shard_map/jit(_pad)/pad | solution.py:411
  3.4 52.0 %shard_map.86 = (f32[2,4,32]{2,1,0:T(4,128)}, f32[2,2,64]{2,1,0:T(2,128)}) custom-call(bf16[512,256]{1,0:T(8,128)(2,1)} %bitcast.14, bf16[2048,256]{1,0:T(8,128)(2,1)} %pad.4.f_in, bf16[4,4096,128]{2,1,0:T(8,128)(2,1)} %bitcast.13, bf16[2,128]{1,0:T(2,128)(2,1)} %desc_in.1, s32[2,2,64]{2,1,0:T(2,128)} %bitcast.17, s32[4,8,16]{2,1,0:T(8,128)} %bitcast.15, ...), custom_call_target="tpu_custom_call" | custom-call | flops 8589934592 | bytes 6000000 | tf_op jit(solution)/shard_map/pallas_call | solution.py:421
  55.4 1.3 %copy.11 = f32[2,4,32]{2,1,0:T(4,128)} copy(f32[2,4,32]{2,1,0:T(4,128)} %get-tuple-element.8) | data formatting | bytes 2048
  56.7 1.2 %copy.12 = f32[2,64,2]{1,2,0:T(2,128)} copy(f32[2,64,2]{1,2,0:T(2,128)} %bitcast.12) | data formatting | bytes 2048

commit v4 on v3

--- a/solution.py
+++ b/solution.py
@@ -21,14 +21,12 @@
     (0, -3), (0, 3), (1, -2), (1, 2), (0, 4), (1, -3), (1, 3), (1, 4),
 )
 EVENTS = {
-    1: (
-        ("near", 1, 0), ("near", 1, 1), ("across", 0), ("fine",), ("near", 2, 0), ("near", 2, 1), ("ready", 1, 0),
-    ),
-    2: (("ready", 0, 1),),
-    3: (("near", 3, 0),),
-    4: (("near", 3, 1), ("across", 1), ("ready", 0, 2)),
-    6: (("ready", 1, 1),),
-    7: (("near", 4, 0), ("across", 2)),
+    1: (("near", 1, 0), ("note", 1), ("near", 1, 1), ("across", 0), ("ready", 1, 0)),
+    2: (("note", 2), ("near", 2, 0), ("near", 2, 1), ("ready", 0, 1)),
+    3: (("note", 3),),
+    4: (("near", 3, 0), ("near", 3, 1), ("across", 1), ("ready", 0, 2)),
+    5: (("fine",),),
+    6: (("near", 4, 0), ("across", 2), ("ready", 1, 1)),
     8: (("ready", 0, 3),),
     10: (("across", 3), ("ready", 1, 2)),
     12: (("ready", 0, 4), ("across", 4)),
@@ -48,11 +46,11 @@
     col_sum = total
     for k in range(9):
         runs = 2 if k < 8 else 1
-        size = 240 if k < 8 else 128
+        size = 240 if k < 8 else 120
         scores = lax.dot_general(
             feat[k * 240 : k * 240 + size, :], query, NT, preferred_element_type=jnp.float32
         )
-        scores = scores[: runs * BLOCK * 8].reshape(runs * BLOCK, 8, rows)
+        scores = scores.reshape(runs * BLOCK, 8, rows)
         new_top = jnp.maximum(top, jnp.max(scores, axis=0))
         keep = jnp.exp2((top - new_top) * SCALE)
         top = new_top
@@ -106,8 +104,8 @@
     mean = jnp.dot(
         mean, pick, preferred_element_type=jnp.float32, precision=lax.Precision.HIGHEST
     ) * (1.0 / 16.0)
-    out[0] = mean[0:4, 0:32] * (1.0 / (GH / 4.0))
-    out[1] = mean[4:8, 0:32] * (1.0 / (GW / 4.0))
+    low = lax.broadcasted_iota(jnp.int32, (8, 128), 0) < 4
+    out[0:8, :] = mean * jnp.where(low, 1.0 / (GH / 4.0), 1.0 / (GW / 4.0))
 
 
 def fine_frames(region, blk, frame_block, lists, valid, gathered, tiles, words, place, fscore, reply):
@@ -189,10 +187,10 @@
 
 
 def kernel(
-    q_in, f_in, tiles_in, desc_in, pos_in, lists, valid,
-    coarse_out, fine_out,
-    queries, feat, tiles, stats_out, stats_in, note, gathered, reply, answers, words, place, fscore,
-    local_sem, near_send, y_recv, z_recv, c_recv, far_send, far_recv,
+    q_in, feat, tiles_in, desc_in, pos_in, lists, valid,
+    out,
+    queries, tiles, stats_out, stats_in, gathered, reply, answers, words, place, fscore,
+    local_sem, near_send, y_recv, z_recv, c_recv, far_send, far_recv, note_recv,
 ):
     blk = lax.axis_index("blk")
     frames = lax.axis_index("frames")
@@ -208,23 +206,22 @@
 
     locals_ = [
         pltpu.make_async_copy(q_in, queries.at[z, yh], local_sem.at[0]),
-        pltpu.make_async_copy(f_in, feat, local_sem.at[1]),
-        pltpu.make_async_copy(tiles_in, tiles, local_sem.at[2]),
+        pltpu.make_async_copy(tiles_in, tiles, local_sem.at[1]),
     ]
     for c in locals_:
         c.start()
 
     barrier = pltpu.get_barrier_semaphore()
 
-    def greet(i, _):
-        pl.semaphore_signal(barrier, inc=1, device_id={"blk": (blk + i) & (PEERS - 1), "frames": frames})
-        pl.semaphore_signal(barrier, inc=1, device_id={"blk": blk, "frames": (frames + i) & (PEERS - 1)})
-        return 0
-
-    lax.fori_loop(1, PEERS, greet, 0)
-    pl.semaphore_signal(barrier, inc=1, device_id=cross)
-
-    note[...] = jnp.zeros_like(note)
+    def partner(bit):
+        return {"blk": blk, "frames": frames + (1 << bit) - 2 * (frames & (1 << bit))}
+
+    neighbours = [{"blk": yh * RING + ring(way), "frames": frames} for way in (1, -1)]
+    for to in [cross, *neighbours, *(partner(bit) for bit in range(4))]:
+        pl.semaphore_signal(barrier, inc=1, device_id=to)
+
+    note = gathered.at[frames]
+    note[...] = jnp.zeros((8, 128), jnp.float32)
     note[0:2, :] = desc_in[...].astype(jnp.float32)
     note[2:4, 0:64] = pos_in[0].astype(jnp.float32)
     note[4:6, 0:64] = pos_in[1].astype(jnp.float32)
@@ -268,11 +265,13 @@
 
     Z_PARTS = [(w, d, c) for w in range(2) for d in range(1, 5) for c in range(2) if d < 4 or c == w]
 
-    def note_copy(i):
-        return remote(
-            note, gathered.at[frames], far_send.at[0], far_recv.at[0],
-            {"blk": blk, "frames": (frames + i) & (PEERS - 1)},
-        )
+    def note_copy(step):
+        ref = gathered.at[pl.ds((frames >> step) << step, 1 << step)]
+        return remote(ref, ref, far_send.at[0], note_recv.at[step], partner(step))
+
+    def pass_note(step):
+        note_copy(step - 1).wait_recv()
+        note_copy(step).start()
 
     def answer_copy(i):
         to = (frames + i) & (PEERS - 1)
@@ -297,26 +296,21 @@
     def wait_all(ref, sem):
         pltpu.make_async_copy(ref, ref, sem).wait()
 
-    def start_notes(i, _):
-        note_copy(i).start()
-        return 0
-
     def enter():
-        pl.semaphore_wait(barrier, 2 * (PEERS - 1) + 1)
+        pl.semaphore_wait(barrier, 7)
         for chunk in range(2):
             z_copy(0, 1, chunk).start()
             z_copy(1, 1, chunk).start()
         y_copy(0, 0, 0).start()
-        lax.fori_loop(1, PEERS, start_notes, 0)
-        gathered[frames] = note[...]
-
+        note_copy(0).start()
+
+    enter()
     locals_[0].wait()
-    locals_[1].wait()
 
     def fine_stage():
-        locals_[2].wait()
-
-        wait_all(gathered.at[1:PEERS], far_recv.at[0])
+        locals_[1].wait()
+
+        note_copy(3).wait_recv()
         fine_frames(
             510, blk, frames, lists, valid, gathered, tiles, words, place, fscore, reply
         )
@@ -360,15 +354,11 @@
             c_copy(chain, 1, stage).wait_recv()
 
     def group_step(i, _):
-        @pl.when(i == 0)
-        def _():
-            enter()
-
         for when, events in EVENTS.items():
             @pl.when(i == when)
             def _(events=events):
                 for event, *at in events:
-                    {"near": near, "across": across, "ready": ready, "fine": fine_stage}[event](*at)
+                    {"near": near, "across": across, "ready": ready, "fine": fine_stage, "note": pass_note}[event](*at)
 
         gz, gy = group_of(i)
         first, second = coarse_group(queries[gz, gy], feat, blk * 17)
@@ -390,10 +380,8 @@
 
     wait_all(answers.at[1:PEERS], far_recv.at[1])
     wait_all(stats_in.at[1:PEERS], far_recv.at[2])
-    coarse_combine(stats_in, coarse_out)
-    answer = jnp.sum(answers[...], axis=0)
-    fine_out[0] = answer[0:2, 0:64]
-    fine_out[1] = answer[2:4, 0:64]
+    coarse_combine(stats_in, out)
+    out[8:16, :] = jnp.sum(answers[...], axis=0)
 
     wait_all(gathered.at[1:PEERS], far_send.at[0])
     wait_all(answers.at[1:PEERS], far_send.at[1])
@@ -408,7 +396,6 @@
     frames_here, region, _ = coarse_feat.shape
     queries = coarse_query.reshape(track_group * heads, channels)
     feat = jnp.transpose(coarse_feat, (1, 0, 2)).reshape(region * frames_here, channels)
-    feat = jnp.pad(feat, ((0, 8), (0, 0)))
     tiles = fine_tiles.reshape(frames_here, -1, fine_tiles.shape[-1])
     pos = jnp.transpose(track_pos, (0, 2, 1))
     lists = jnp.transpose(tile_list[:, 0], (0, 2, 1))
@@ -418,34 +405,30 @@
     far = pl.BlockSpec(memory_space=pl.ANY)
     dma = pltpu.SemaphoreType.DMA
     rows = queries.shape[0]
-    coarse_pos, offset = pl.pallas_call(
+    packed = pl.pallas_call(
         kernel,
-        out_shape=(
-            jax.ShapeDtypeStruct((2, 4, 32), f32),
-            jax.ShapeDtypeStruct((2, 2, 64), f32),
-        ),
-        in_specs=[far, far, far, vmem, vmem, vmem, vmem],
-        out_specs=(vmem, vmem),
+        out_shape=jax.ShapeDtypeStruct((16, 128), f32),
+        in_specs=[far, vmem, far, vmem, vmem, vmem, vmem],
+        out_specs=vmem,
         scratch_shapes=[
             pltpu.VMEM((RING, 2, rows, channels), jnp.bfloat16),
-            pltpu.VMEM(feat.shape, jnp.bfloat16),
             pltpu.VMEM(tiles.shape, jnp.bfloat16),
             pltpu.VMEM((PEERS, 2, 8, rows), f32),
             pltpu.VMEM((PEERS, 2, 8, rows), f32),
-            pltpu.VMEM((8, 128), f32),
             pltpu.VMEM((PEERS, 8, 128), f32),
             pltpu.VMEM((PEERS, 8, 128), f32),
             pltpu.VMEM((PEERS, 8, 128), f32),
             pltpu.VMEM((128, 128), f32),
             pltpu.VMEM((2, 32, 128), f32),
             pltpu.VMEM((32, 32, 128), f32),
-            dma((3,)),
+            dma((2,)),
             dma((3,)),
             dma((2, 9)),
             dma((2, 8)),
             dma((15,)),
             dma((3,)),
             dma((3,)),
+            dma((4,)),
         ],
         compiler_params=pltpu.CompilerParams(
             collective_id=0, has_side_effects=True, vmem_limit_bytes=56 * 2**20
@@ -454,6 +437,8 @@
             flops=2 * 8192 * 2048 * 256, bytes_accessed=6 * 10**6, transcendentals=8192 * 2048
         ),
     )(queries, feat, tiles, fine_query, pos, lists, valid)
+    coarse_pos = packed[0:8, 0:32].reshape(2, 4, 32)
+    offset = packed[8:12, 0:64].reshape(2, 2, 64)
     return coarse_pos, jnp.transpose(offset, (0, 2, 1))
 
 

time: 58.2 us -> 59.5 us (1.022)
  the two profiles are of different devices: /device:TPU:14 before, /device:TPU:1 now
where the time goes in v4:
time: 59.5 us; the launch traced here: 59.3 us
  Pallas kernels  53.6 us (90%)
  local copies, waits for them, and re-layouts  5.04 us (8%)
  between operations  0.64 us (1%)
    pallas_call x1, Pallas kernels, body(): pl.pallas_call(kernel, out_shape=jax.ShapeDtypeStruct((16, 128), f32), in...  53.6 us
    reshape x1, local copies, waits for them, and re-layouts, body(): jnp.transpose(coarse_feat, (1, 0, 2))  2.52 us
    slice x1, local copies, waits for them, and re-layouts, body(): coarse_pos = packed[0:8, 0:32].reshape(2, 4, 32)  1.27 us
    slice x1, local copies, waits for them, and re-layouts, body(): offset = packed[8:12, 0:64].reshape(2, 2, 64)  1.25 us

profile of v4, /device:TPU:1, one launch (start us, length us, event | category | flops | bytes accessed | tf_op | source)
XLA Modules:
  0.0 59.3 jit_solution(17403484873939525148)
XLA Ops:
  0.6 2.5 %reshape.20.feat = bf16[2040,256]{1,0:T(8,128)(2,1)} reshape(bf16[510,4,256]{2,1,0:T(4,128)(2,1)} %bitcast.14) | data formatting | bytes 2088960 | tf_op jit(solution)/shard_map/reshape | solution.py:398
  3.1 53.6 %shard_map.86 = f32[16,128]{1,0:T(8,128)} custom-call(bf16[512,256]{1,0:T(8,128)(2,1)} %bitcast.18, bf16[2040,256]{1,0:T(8,128)(2,1)} %reshape.20.feat, bf16[4,4096,128]{2,1,0:T(8,128)(2,1)} %bitcast.17, bf16[2,128]{1,0:T(2,128)(2,1)} %desc_in.1, s32[2,2,64]{2,1,0:T(2,128)} %bitcast.21, s32[4,8,16]{2,1,0:T(8,128)} %bitcast.19, s32[4,8,16]{2,1,0:T(8,128)} %bitcast.20), custom_call_target="tpu_custom_call" | custom-call | flops 8589934592 | bytes 6000000 | tf_op jit(solution)/shard_map/pallas_call | solution.py:408
  56.8 1.3 %slice.7 = f32[4,64]{1,0:T(4,128)} slice(f32[16,128]{1,0:T(8,128)} %shard_map.86), slice={[8:12], [0:64]} | slice | bytes 2048 | tf_op jit(solution)/shard_map/slice | solution.py:441
  58.0 1.3 %slice.6 = f32[8,32]{1,0:T(8,128)} slice(f32[16,128]{1,0:T(8,128)} %shard_map.86), slice={[0:8], [0:32]} | slice | bytes 2048 | tf_op jit(solution)/shard_map/slice | solution.py:440

commit v5 on v3

--- a/solution.py
+++ b/solution.py
@@ -48,11 +48,11 @@
     col_sum = total
     for k in range(9):
         runs = 2 if k < 8 else 1
-        size = 240 if k < 8 else 128
+        size = 240 if k < 8 else 120
         scores = lax.dot_general(
             feat[k * 240 : k * 240 + size, :], query, NT, preferred_element_type=jnp.float32
         )
-        scores = scores[: runs * BLOCK * 8].reshape(runs * BLOCK, 8, rows)
+        scores = scores.reshape(runs * BLOCK, 8, rows)
         new_top = jnp.maximum(top, jnp.max(scores, axis=0))
         keep = jnp.exp2((top - new_top) * SCALE)
         top = new_top
@@ -106,8 +106,8 @@
     mean = jnp.dot(
         mean, pick, preferred_element_type=jnp.float32, precision=lax.Precision.HIGHEST
     ) * (1.0 / 16.0)
-    out[0] = mean[0:4, 0:32] * (1.0 / (GH / 4.0))
-    out[1] = mean[4:8, 0:32] * (1.0 / (GW / 4.0))
+    low = lax.broadcasted_iota(jnp.int32, (8, 128), 0) < 4
+    out[0:8, :] = mean * jnp.where(low, 1.0 / (GH / 4.0), 1.0 / (GW / 4.0))
 
 
 def fine_frames(region, blk, frame_block, lists, valid, gathered, tiles, words, place, fscore, reply):
@@ -190,8 +190,8 @@
 
 def kernel(
     q_in, f_in, tiles_in, desc_in, pos_in, lists, valid,
-    coarse_out, fine_out,
-    queries, feat, tiles, stats_out, stats_in, note, gathered, reply, answers, words, place, fscore,
+    out,
+    queries, raw, feat, tiles, stats_out, stats_in, gathered, reply, answers, words, place, fscore,
     local_sem, near_send, y_recv, z_recv, c_recv, far_send, far_recv,
 ):
     blk = lax.axis_index("blk")
@@ -208,8 +208,8 @@
 
     locals_ = [
         pltpu.make_async_copy(q_in, queries.at[z, yh], local_sem.at[0]),
-        pltpu.make_async_copy(f_in, feat, local_sem.at[1]),
-        pltpu.make_async_copy(tiles_in, tiles, local_sem.at[2]),
+        pltpu.make_async_copy(tiles_in, tiles, local_sem.at[1]),
+        pltpu.make_async_copy(f_in, raw, local_sem.at[2]),
     ]
     for c in locals_:
         c.start()
@@ -224,7 +224,8 @@
     lax.fori_loop(1, PEERS, greet, 0)
     pl.semaphore_signal(barrier, inc=1, device_id=cross)
 
-    note[...] = jnp.zeros_like(note)
+    note = gathered.at[frames]
+    note[...] = jnp.zeros((8, 128), jnp.float32)
     note[0:2, :] = desc_in[...].astype(jnp.float32)
     note[2:4, 0:64] = pos_in[0].astype(jnp.float32)
     note[4:6, 0:64] = pos_in[1].astype(jnp.float32)
@@ -270,7 +271,7 @@
 
     def note_copy(i):
         return remote(
-            note, gathered.at[frames], far_send.at[0], far_recv.at[0],
+            note, note, far_send.at[0], far_recv.at[0],
             {"blk": blk, "frames": (frames + i) & (PEERS - 1)},
         )
 
@@ -308,13 +309,16 @@
             z_copy(1, 1, chunk).start()
         y_copy(0, 0, 0).start()
         lax.fori_loop(1, PEERS, start_notes, 0)
-        gathered[frames] = note[...]
-
+
+    enter()
+    locals_[2].wait()
+    for cells in range(0, 510, 60):
+        size = min(60, 510 - cells)
+        feat[cells * 4 : (cells + size) * 4, :] = raw[cells : cells + size].reshape(size * 4, 256)
     locals_[0].wait()
-    locals_[1].wait()
 
     def fine_stage():
-        locals_[2].wait()
+        locals_[1].wait()
 
         wait_all(gathered.at[1:PEERS], far_recv.at[0])
         fine_frames(
@@ -360,10 +364,6 @@
             c_copy(chain, 1, stage).wait_recv()
 
     def group_step(i, _):
-        @pl.when(i == 0)
-        def _():
-            enter()
-
         for when, events in EVENTS.items():
             @pl.when(i == when)
             def _(events=events):
@@ -390,10 +390,8 @@
 
     wait_all(answers.at[1:PEERS], far_recv.at[1])
     wait_all(stats_in.at[1:PEERS], far_recv.at[2])
-    coarse_combine(stats_in, coarse_out)
-    answer = jnp.sum(answers[...], axis=0)
-    fine_out[0] = answer[0:2, 0:64]
-    fine_out[1] = answer[2:4, 0:64]
+    coarse_combine(stats_in, out)
+    out[8:16, :] = jnp.sum(answers[...], axis=0)
 
     wait_all(gathered.at[1:PEERS], far_send.at[0])
     wait_all(answers.at[1:PEERS], far_send.at[1])
@@ -403,12 +401,17 @@
     wait_all(queries.at[:, 0, 0:480], near_send.at[2])
 
 
+def split_result(packed, coarse_pos, offset):
+    for i in range(2):
+        coarse_pos[i] = packed[4 * i : 4 * i + 4, 0:32]
+        offset[i] = packed[8 + 2 * i : 10 + 2 * i, 0:64]
+
+
 def body(coarse_query, coarse_feat, fine_query, fine_tiles, track_pos, tile_list, tile_valid):
     track_group, heads, channels = coarse_query.shape
     frames_here, region, _ = coarse_feat.shape
     queries = coarse_query.reshape(track_group * heads, channels)
-    feat = jnp.transpose(coarse_feat, (1, 0, 2)).reshape(region * frames_here, channels)
-    feat = jnp.pad(feat, ((0, 8), (0, 0)))
+    feat = jnp.transpose(coarse_feat, (1, 0, 2))
     tiles = fine_tiles.reshape(frames_here, -1, fine_tiles.shape[-1])
     pos = jnp.transpose(track_pos, (0, 2, 1))
     lists = jnp.transpose(tile_list[:, 0], (0, 2, 1))
@@ -418,21 +421,18 @@
     far = pl.BlockSpec(memory_space=pl.ANY)
     dma = pltpu.SemaphoreType.DMA
     rows = queries.shape[0]
-    coarse_pos, offset = pl.pallas_call(
+    packed = pl.pallas_call(
         kernel,
-        out_shape=(
-            jax.ShapeDtypeStruct((2, 4, 32), f32),
-            jax.ShapeDtypeStruct((2, 2, 64), f32),
-        ),
+        out_shape=jax.ShapeDtypeStruct((16, 128), f32),
         in_specs=[far, far, far, vmem, vmem, vmem, vmem],
-        out_specs=(vmem, vmem),
+        out_specs=vmem,
         scratch_shapes=[
             pltpu.VMEM((RING, 2, rows, channels), jnp.bfloat16),
             pltpu.VMEM(feat.shape, jnp.bfloat16),
+            pltpu.VMEM((region * frames_here, channels), jnp.bfloat16),
             pltpu.VMEM(tiles.shape, jnp.bfloat16),
             pltpu.VMEM((PEERS, 2, 8, rows), f32),
             pltpu.VMEM((PEERS, 2, 8, rows), f32),
-            pltpu.VMEM((8, 128), f32),
             pltpu.VMEM((PEERS, 8, 128), f32),
             pltpu.VMEM((PEERS, 8, 128), f32),
             pltpu.VMEM((PEERS, 8, 128), f32),
@@ -454,6 +454,15 @@
             flops=2 * 8192 * 2048 * 256, bytes_accessed=6 * 10**6, transcendentals=8192 * 2048
         ),
     )(queries, feat, tiles, fine_query, pos, lists, valid)
+    coarse_pos, offset = pl.pallas_call(
+        split_result,
+        out_shape=(
+            jax.ShapeDtypeStruct((2, 4, 32), f32),
+            jax.ShapeDtypeStruct((2, 2, 64), f32),
+        ),
+        in_specs=[vmem],
+        out_specs=(vmem, vmem),
+    )(packed)
     return coarse_pos, jnp.transpose(offset, (0, 2, 1))
 
 

time: 58.2 us -> 54.3 us (0.933)
  local copies, waits for them, and re-layouts: 5.28 us -> 0 us
  Pallas kernels: 52 us -> 53.4 us
    unnamed x2 -> x0, local copies, waits for them, and re-layouts: 2.5 us -> none
    reshape x1 -> x0, local copies, waits for them, and re-layouts: 1.72 us -> none  [body(): jnp.transpose(coarse_feat, (1, 0, 2))]
    pallas_call x1 -> x2, Pallas kernels: 52 us -> 53.4 us  [the longest x1 52.1 us: body(): pl.pallas_call(kernel, out_shape=jax.ShapeDtypeStruct((16, 128), f32), in...]
    pad x1 -> x0, local copies, waits for them, and re-layouts: 1.06 us -> none  [body(): feat = jnp.pad(feat, ((0, 8), (0, 0)))]
where the time goes in v5:
time: 54.3 us; the launch traced here: 54 us
  Pallas kernels  53.4 us (98%)
  between operations  0.64 us (1%)
    pallas_call x1, Pallas kernels, body(): pl.pallas_call(kernel, out_shape=jax.ShapeDtypeStruct((16, 128), f32), in...  52.1 us
    pallas_call x1, Pallas kernels, body(): pl.pallas_call(split_result, out_shape=(jax.ShapeDtypeStruct((2, 4, 32),...  1.29 us

profile of v5, /device:TPU:14, one launch (start us, length us, event | category | flops | bytes accessed | tf_op | source)
XLA Modules:
  0.0 54.0 jit_solution(13306084652234636838)
XLA Ops:
  0.6 52.1 %shard_map.86.packed = f32[16,128]{1,0:T(8,128)} custom-call(bf16[512,256]{1,0:T(8,128)(2,1)} %bitcast.13, bf16[510,4,256]{2,1,0:T(4,128)(2,1)} %bitcast.12, bf16[4,4096,128]{2,1,0:T(8,128)(2,1)} %bitcast.11, bf16[2,128]{1,0:T(2,128)(2,1)} %desc_in.1, s32[2,2,64]{2,1,0:T(2,128)} %bitcast.16, s32[4,8,16]{2,1,0:T(8,128)} %bitcast.14, s32[4,8,16]{2,1,0:T(8,128)} %bitcast.15), custom_call_target="tpu_custom_call" | custom-call | flops 8589934592 | bytes 6000000 | tf_op jit(solution)/shard_map/pallas_call | solution.py:424
  52.7 1.3 %shard_map.87 = (f32[2,4,32]{2,1,0:T(4,128)}, f32[2,2,64]{2,1,0:T(2,128)}) custom-call(f32[16,128]{1,0:T(8,128)} %shard_map.86.packed), custom_call_target="tpu_custom_call" | custom-call | tf_op jit(solution)/shard_map/pallas_call | solution.py:457

commit v6 on v5

--- a/solution.py
+++ b/solution.py
@@ -30,9 +30,10 @@
     6: (("ready", 1, 1),),
     7: (("near", 4, 0), ("across", 2)),
     8: (("ready", 0, 3),),
-    10: (("across", 3), ("ready", 1, 2)),
-    12: (("ready", 0, 4), ("across", 4)),
-    13: (("ready", 1, 3),),
+    10: (("ready", 1, 2),),
+    11: (("across", 3),),
+    12: (("ready", 0, 4),),
+    13: (("across", 4), ("ready", 1, 3)),
     15: (("ready", 1, 4),),
 }
 SCALE = math.log2(math.e) / 16.0

time: 54.3 us -> 53 us (0.976)
  Pallas kernels: 53.4 us -> 51.8 us
    pallas_call x1, Pallas kernels: 52.1 us -> 50.5 us  [body(): pl.pallas_call(kernel, out_shape=jax.ShapeDtypeStruct((16, 128), f32), in...]
where the time goes in v6:
time: 53 us; the launch traced here: 52.4 us
  Pallas kernels  51.8 us (98%)
  between operations  0.64 us (1%)
    pallas_call x1, Pallas kernels, body(): pl.pallas_call(kernel, out_shape=jax.ShapeDtypeStruct((16, 128), f32), in...  50.5 us
    pallas_call x1, Pallas kernels, body(): pl.pallas_call(split_result, out_shape=(jax.ShapeDtypeStruct((2, 4, 32),...  1.29 us

profile of v6, /device:TPU:14, one launch (start us, length us, event | category | flops | bytes accessed | tf_op | source)
XLA Modules:
  0.0 52.4 jit_solution(18116415374129506148)
XLA Ops:
  0.6 50.5 %shard_map.86.packed = f32[16,128]{1,0:T(8,128)} custom-call(bf16[512,256]{1,0:T(8,128)(2,1)} %bitcast.13, bf16[510,4,256]{2,1,0:T(4,128)(2,1)} %bitcast.12, bf16[4,4096,128]{2,1,0:T(8,128)(2,1)} %bitcast.11, bf16[2,128]{1,0:T(2,128)(2,1)} %desc_in.1, s32[2,2,64]{2,1,0:T(2,128)} %bitcast.16, s32[4,8,16]{2,1,0:T(8,128)} %bitcast.14, s32[4,8,16]{2,1,0:T(8,128)} %bitcast.15), custom_call_target="tpu_custom_call" | custom-call | flops 8589934592 | bytes 6000000 | tf_op jit(solution)/shard_map/pallas_call | solution.py:425
  51.1 1.3 %shard_map.87 = (f32[2,4,32]{2,1,0:T(4,128)}, f32[2,2,64]{2,1,0:T(2,128)}) custom-call(f32[16,128]{1,0:T(8,128)} %shard_map.86.packed), custom_call_target="tpu_custom_call" | custom-call | tf_op jit(solution)/shard_map/pallas_call | solution.py:458
